TPU v7x, 32 devices: a whole 2x2x4 slice. The times are simulated.
32 devices in a mesh: dp: 32 (over z, y, x, core).
Axes of the slice: x: 2, y: 2, z: 4, core: 2. Of those that a mesh axis runs over, the one named last changes fastest.
Arguments:
- tokens: bfloat16 [64, 512, 512], P('dp'), may hold values from -6 to 6
- memory: bfloat16 [64, 512, 512], P('dp'), may hold values from -6 to 6
- segments: int32 [64, 512], P('dp'), may hold values from 0 to 3, never falling along the last dimension, each value on 1 to 256 neighbouring positions
- cotangent: bfloat16 [64, 512, 512], P('dp'), may hold values from -6 to 6
- group_sizes: int32 [8], replicated, may hold values from 1 to 8, 32 in all
- task_embed: bfloat16 [8, 64], replicated, may hold values from -4 to 4
- position_embed: bfloat16 [2, 64], replicated, may hold values from -4 to 4
- hyper_first: bfloat16 [64, 128], replicated, may hold values from -0.75 to 0.75
- hyper_second: bfloat16 [128, 64], replicated, may hold values from -0.5 to 0.5
- hyper_gain: bfloat16 [64, 1536], replicated, may hold values from -0.375 to 0.375
- hyper_down: bfloat16 [64, 8192], replicated, may hold values from -0.03125 to 0.03125
- hyper_up: bfloat16 [64, 8192], replicated, may hold values from -0.1875 to 0.1875
- self_qkv: bfloat16 [3, 512, 512], replicated, may hold values from -0.25 to 0.25
- self_out: bfloat16 [512, 512], replicated, may hold values from -0.75 to 0.75
- cross_qkv: bfloat16 [3, 512, 512], replicated, may hold values from -0.25 to 0.25
- cross_out: bfloat16 [512, 512], replicated, may hold values from -1.5 to 1.5
- ffn_in: bfloat16 [512, 2048], replicated, may hold values from -0.25 to 0.25
- ffn_out: bfloat16 [2048, 512], replicated, may hold values from -0.125 to 0.125
Outputs:
- output: bfloat16 [64, 512, 512], P('dp')
- input_grad: float32 [64, 512, 512], P('dp')
- memory_grad: float32 [64, 512, 512], P('dp')
- task_grad: float32 [8, 64], replicated
- position_grad: float32 [2, 64], replicated
- hyper_first_grad: float32 [64, 128], replicated
- hyper_second_grad: float32 [128, 64], replicated
- hyper_gain_grad: float32 [64, 1536], replicated
- hyper_down_grad: float32 [64, 8192], replicated
- hyper_up_grad: float32 [64, 8192], replicated
- self_qkv_grad: float32 [3, 512, 512], replicated
- self_out_grad: float32 [512, 512], replicated
- cross_qkv_grad: float32 [3, 512, 512], replicated
- cross_out_grad: float32 [512, 512], replicated
- ffn_in_grad: float32 [512, 2048], replicated
- ffn_out_grad: float32 [2048, 512], replicated
Inputs may be any that keep to these rules, and one draw needn't show every extreme that they name: The devices of dp belong to tasks in order: the first group_sizes[0] devices to task 0, the next group_sizes[1] to task 1, and so on; the sizes add up to 32. `segments`: along each row the segment numbers never fall; every segment holds at most 256 positions.
All inputs are finite; a program needn't handle non-finite values.
Results may differ from a plain program's by a relative error of at most 0.024.
Values sent between devices are 32-bit elements; how exact they have to be, the bound alone decides.
No kernel may reach another device: no remote copies, remote signals or barrier semaphores. Data moves between devices by JAX's collectives and lax.ppermute only.
A program may use at most 192 MiB of HBM per device.

v0:
```python
import functools

import jax
import jax.numpy as jnp
from jax import lax
from jax.experimental import pallas as pl
from jax.experimental.pallas import tpu as pltpu
from jax.sharding import PartitionSpec as P

PAIRS = 4
LANES = 128
RANK = 16
LOG2E = 1.4426950408889634
epsilon = 1e-06
highest = lax.Precision.HIGHEST
f32 = jnp.float32
bf16 = jnp.bfloat16
SHORT = pl.CostEstimate(flops=1, bytes_accessed=1, transcendentals=0)


def dot(left, right):
    return jnp.dot(left, right, preferred_element_type=f32)


def dot_nt(left, right):
    return lax.dot_general(left, right, (((1,), (1,)), ((), ())), preferred_element_type=f32)


def dot_tn(left, right):
    return lax.dot_general(left, right, (((0,), (0,)), ((), ())), preferred_element_type=f32)


def three(values):
    high = values.astype(bf16)
    rest = values - high.astype(f32)
    mid = rest.astype(bf16)
    return high, mid, (rest - mid.astype(f32)).astype(bf16)


def dot_exact(values, table):
    high, mid, low = three(values)
    return dot(high, table) + (dot(mid, table) + dot(low, table))


def dot_exact_nt(values, table):
    high, mid, low = three(values)
    return dot_nt(high, table) + (dot_nt(mid, table) + dot_nt(low, table))


def rms_back(values, inv, gain, grad):
    unit = values * inv
    scaled = grad * gain
    mean = jnp.mean(scaled * unit, axis=-1, keepdims=True)
    return inv * (scaled - unit * mean), jnp.sum(grad * unit, axis=0, keepdims=True)


def rms_inv(values):
    return lax.rsqrt(jnp.mean(values * values, axis=-1, keepdims=True) + epsilon)


def low_lanes():
    return lax.broadcasted_iota(jnp.int32, (1, LANES), 1) < 64


def silu_back(values, grad):
    gate = lax.logistic(values)
    return grad * (gate * (1.0 + values * (1.0 - gate)))


def task_place(sizes_ref, count, place):
    end, task = jnp.int32(0), jnp.int32(0)
    for i in range(count):
        end = end + sizes_ref[i]
        task = task + jnp.where(end <= place, 1, 0)
    size = sizes_ref[0]
    for i in range(1, count):
        size = jnp.where(task == i, sizes_ref[i], size)
    return task, size


def pick_row(table, task):
    rows = lax.broadcasted_iota(jnp.int32, table.shape, 0)
    return jnp.sum(jnp.where(rows == task, table, 0.0), axis=0, keepdims=True)


def fold_tables():
    feature = lax.broadcasted_iota(jnp.int32, (512, 64), 0)
    block = lax.broadcasted_iota(jnp.int32, (512, 64), 1)
    expand = jnp.where(feature // 8 == block, 1.0, 0.0).astype(bf16)
    feature = lax.broadcasted_iota(jnp.int32, (512, LANES), 0)
    lane = lax.broadcasted_iota(jnp.int32, (512, LANES), 1)
    own = (lane // RANK) == (feature % 8)
    row = lax.broadcasted_iota(jnp.int32, (LANES, LANES), 0)
    lane = lax.broadcasted_iota(jnp.int32, (LANES, LANES), 1)
    fold = jnp.where((row % RANK) == lane, 1.0, 0.0).astype(bf16)
    return expand, own, fold


def upper(place, bits):
    return lax.rem(jnp.where(lax.rem(place, 2) == 1, place // bits[1], place // bits[0]), 2)


def halves(total_ref, kept_ref, sent_ref, sem, base):
    half = total_ref.shape[0] // 2
    side = lax.rem(lax.axis_index("dp"), 2)
    return (
        pltpu.make_async_copy(total_ref.at[pl.ds(pl.multiple_of((1 - side) * half, half), half)], sent_ref, sem.at[base]),
        pltpu.make_async_copy(total_ref.at[pl.ds(pl.multiple_of(side * half, half), half)], kept_ref, sem.at[base + 1]),
    )


def attend_block(pair_q, keys, values_ones, bias):
    low = low_lanes()
    probs, mixed = [], []
    for head in range(2):
        own = low if head == 0 else jnp.logical_not(low)
        scores = dot_nt(jnp.where(own, pair_q, jnp.zeros_like(pair_q)), keys)
        if bias is not None:
            scores = scores + bias
        top = jnp.max(scores, axis=-1, keepdims=True)
        prob = jnp.exp2((scores - top) * LOG2E).astype(bf16)
        probs.append(prob)
        mixed.append(dot(prob, values_ones))
    total = jnp.where(low, mixed[0][:, LANES:], mixed[1][:, LANES:])
    share = 1.0 / total
    out = jnp.where(low, mixed[0][:, :LANES], mixed[1][:, :LANES]) * share
    return probs, out.astype(bf16), share


def hyper_tables(task, embed_ref, position_ref, first_ref, second_ref, gain_ref, down_ref, up_ref,
                 gains_ref, down_w_ref, up_w_ref, pre_ref, code_ref, flat_ref):
    pre = dot(embed_ref[...], first_ref[...])
    code = dot_exact_nt(pre * lax.logistic(pre), second_ref[...])
    pre_ref[...] = pre
    code_ref[...] = code
    own = pick_row(code, task)
    gain = dot_exact(jnp.broadcast_to(own, (8, own.shape[1])), gain_ref[...])
    for i in range(3):
        gains_ref[i] = 1.0 + gain[:, i * 512 : (i + 1) * 512]
    rows = lax.broadcasted_iota(jnp.int32, (8, own.shape[1]), 0)
    position = position_ref[...].astype(f32)
    codes = own + jnp.where(rows == 0, position[0:1], position[1:2])
    expand, mine, fold = fold_tables()
    flat = dot_exact(codes, down_ref[...])
    for p in range(2):
        for a in range(64):
            flat_ref[a : a + 1, :] = flat[p : p + 1, a * LANES : (a + 1) * LANES]
        spread = jnp.where(mine, dot(expand, flat_ref[...].astype(bf16)), 0.0)
        down_w_ref[p] = dot(spread.astype(bf16), fold).astype(bf16)
    flat = dot_exact(codes, up_ref[...])
    for p in range(2):
        flat_ref[...] = jnp.zeros_like(flat_ref)
        wide = []
        for a in range(RANK):
            wide.append(flat[p : p + 1, a * 512 : (a + 1) * 512])
        wide.append(jnp.zeros((LANES - RANK, 512), f32))
        up_w_ref[p] = jnp.concatenate(wide, axis=0).astype(bf16)


def forward_kernel(
    total_devices, ntask,
    sizes_ref, x_ref, mem_ref, seg_ref, cot_ref,
    embed_ref, position_ref, first_ref, second_ref, hgain_ref, hdown_ref, hup_ref,
    self_qkv_ref, self_out_ref, cross_qkv_ref, cross_out_ref, ffn_in_ref, ffn_out_ref,
    output_ref, grad_two_ref, in_kept_ref, in_sent_ref, out_kept_ref, out_sent_ref, up_grad_ref, down_grad_ref, gain_grad_ref,
    gains_ref, down_w_ref, up_w_ref, pre_ref, code_ref,
    in_one_ref, q_ref, k_ref, v_ref, share_one_ref, mixed_one_ref, branch_ref, narrow_ref, after_one_ref,
    in_two_ref, cq_ref, ck_ref, cv_ref, share_two_ref, mixed_two_ref, prob_one_ref, prob_two_ref,
    flat_ref, bias_ref, slot_ref, sem, inner_act_ref, slope_ref, after_two_ref,
    ffn_in_grad_ref, ffn_out_grad_ref, part_sem,
):
    row = pl.program_id(0)
    place = lax.axis_index("dp")
    task, size = task_place(sizes_ref, ntask, place)

    @pl.when(row == 0)
    def _():
        hyper_tables(task, embed_ref, position_ref, first_ref, second_ref, hgain_ref, hdown_ref, hup_ref,
                     gains_ref, down_w_ref, up_w_ref, pre_ref, code_ref, flat_ref)

    x = x_ref[0].astype(f32)
    in_one = (x * rms_inv(x) * gains_ref[0, 0:1]).astype(bf16)
    in_one_ref[0] = in_one
    q_ref[0] = (dot(in_one, self_qkv_ref[0]).astype(bf16).astype(f32) * 0.125).astype(bf16)
    k_ref[0] = dot(in_one, self_qkv_ref[1]).astype(bf16)
    v_ref[0] = dot(in_one, self_qkv_ref[2]).astype(bf16)
    memory = mem_ref[0]
    ck_ref[0] = dot(memory, cross_qkv_ref[1]).astype(bf16)
    cv_ref[0] = dot(memory, cross_qkv_ref[2]).astype(bf16)
    queries = lax.broadcasted_iota(jnp.int32, (512, 512), 0)
    keys = lax.broadcasted_iota(jnp.int32, (512, 512), 1)
    segment = seg_ref[pl.ds(row, 1), :].astype(f32)
    segment_q = jnp.broadcast_to(segment, (LANES, segment.shape[1])).T[:, 0:1]
    allowed = jnp.logical_and(keys <= queries, segment_q == segment)
    bias_ref[...] = jnp.where(allowed, 0.0, -1e9)

    def attend_row(q_ref, k_ref, v_ref, masked, mixed_ref, share_ref, prob_ref):
        copies = []
        for pair in range(PAIRS):
            lanes = slice(pair * LANES, (pair + 1) * LANES)
            slot = pair % 2
            if pair >= 2:
                copies[pair - 2].wait()
            pair_k = k_ref[0, :, lanes]
            pair_v = v_ref[0, :, lanes]
            ones = jnp.concatenate([pair_v, jnp.ones_like(pair_v)], axis=1)
            for block in range(2):
                rows = slice(block * 256, (block + 1) * 256)
                span = (block + 1) * 256 if masked else 512
                probs, mixed, share = attend_block(
                    q_ref[0, rows, lanes], pair_k[:span], ones[:span],
                    bias_ref[rows, :span] if masked else None,
                )
                for head in range(2):
                    slot_ref[slot, head, rows, :span] = probs[head]
                mixed_ref[0, rows, lanes] = mixed
                share_ref[0, rows, lanes] = share
            copy = pltpu.make_async_copy(
                slot_ref.at[slot], prob_ref.at[row, pl.ds(pair * 2, 2)], sem.at[slot]
            )
            copy.start()
            copies.append(copy)
        copies[PAIRS - 2].wait()
        copies[PAIRS - 1].wait()

    attend_row(q_ref, k_ref, v_ref, True, mixed_one_ref, share_one_ref, prob_one_ref)

    branch = dot(mixed_one_ref[0], self_out_ref[...])
    branch_low = branch.astype(bf16)
    branch_ref[0] = branch_low
    narrow = dot(branch_low, down_w_ref[0])
    narrow_ref[0] = narrow
    narrow_act = (narrow * lax.logistic(narrow)).astype(bf16)
    after_one = x_ref[0].astype(f32) + branch + dot(narrow_act, up_w_ref[0])
    after_one_ref[0] = after_one
    in_two = (after_one * rms_inv(after_one) * gains_ref[1, 0:1]).astype(bf16)
    in_two_ref[0] = in_two
    cq_ref[0] = (dot(in_two, cross_qkv_ref[0]).astype(bf16).astype(f32) * 0.125).astype(bf16)

    attend_row(cq_ref, ck_ref, cv_ref, False, mixed_two_ref, share_two_ref, prob_two_ref)

    after_two = after_one_ref[0] + dot(mixed_two_ref[0], cross_out_ref[...])
    after_two_ref[...] = after_two
    in_three = (after_two * rms_inv(after_two) * gains_ref[2, 0:1]).astype(bf16)
    outer = None
    for c in range(4):
        cols = slice(c * 512, (c + 1) * 512)
        inner = dot(in_three, ffn_in_ref[:, cols])
        phi = 0.5 * (1.0 + lax.erf(inner * 0.7071067811865476))
        slope_ref[:, cols] = phi + inner * jnp.exp2(inner * inner * (-0.5 * LOG2E)) * 0.3989422804014327
        act = (inner * phi).astype(bf16)
        inner_act_ref[:, cols] = act
        part = dot(act, ffn_out_ref[cols, :])
        outer = part if outer is None else outer + part
    outer_low = outer.astype(bf16)
    narrow = dot(outer_low, down_w_ref[1])
    gate = lax.logistic(narrow)
    narrow_act = (narrow * gate).astype(bf16)
    output_ref[0] = (after_two_ref[...] + outer + dot(narrow_act, up_w_ref[1])).astype(bf16)

    keep = jnp.where(row == 0, 0.0, 1.0)
    share = total_devices / (ntask * size.astype(f32))
    grad = cot_ref[0].astype(f32) * share
    grad_low = grad.astype(bf16)
    d_narrow = (dot_nt(grad_low, up_w_ref[1]) * (gate * (1.0 + narrow * (1.0 - gate)))).astype(bf16)
    d_outer = (grad + dot_nt(d_narrow, down_w_ref[1])).astype(bf16)

    @pl.when(row == 0)
    def _():
        up_grad_ref[...] = jnp.zeros_like(up_grad_ref)
        down_grad_ref[...] = jnp.zeros_like(down_grad_ref)
        gain_grad_ref[...] = jnp.zeros_like(gain_grad_ref)
        ffn_in_grad_ref[...] = jnp.zeros_like(ffn_in_grad_ref)
        ffn_out_grad_ref[...] = jnp.zeros_like(ffn_out_grad_ref)

    up_grad_ref[...] += dot_tn(narrow_act, grad_low)[:RANK]
    down_grad_ref[...] += dot_tn(d_narrow, outer_low)[:RANK]
    for c in range(4):
        cols = slice(c * 512, (c + 1) * 512)
        ffn_out_grad_ref[cols, :] += dot_tn(inner_act_ref[:, cols], d_outer)

    last = row == pl.num_programs(0) - 1

    @pl.when(last)
    def _():
        for copy in halves(ffn_out_grad_ref, out_kept_ref, out_sent_ref, part_sem, 0):
            copy.start()

    in_three_t = in_three.T
    d_in = None
    for c in range(4):
        cols = slice(c * 512, (c + 1) * 512)
        d_inner = (dot_nt(d_outer, ffn_out_ref[cols, :]) * slope_ref[:, cols]).astype(bf16)
        ffn_in_grad_ref[:, cols] += dot(in_three_t, d_inner)
        part = dot_nt(d_inner, ffn_in_ref[:, cols])
        d_in = part if d_in is None else d_in + part

    @pl.when(last)
    def _():
        for copy in halves(ffn_in_grad_ref, in_kept_ref, in_sent_ref, part_sem, 2):
            copy.start()

    after_two = after_two_ref[...]
    d_after, gain_grad = rms_back(after_two, rms_inv(after_two), gains_ref[2, 0:1], d_in)
    grad_two_ref[0] = cot_ref[0].astype(f32) * share + d_after
    gain_grad_ref[...] += jnp.broadcast_to(gain_grad, gain_grad_ref.shape)

    @pl.when(last)
    def _():
        for copy in halves(ffn_out_grad_ref, out_kept_ref, out_sent_ref, part_sem, 0):
            copy.wait()
        for copy in halves(ffn_in_grad_ref, in_kept_ref, in_sent_ref, part_sem, 2):
            copy.wait()


def run_forward(tokens, memory, segments, cotangent, group_sizes, params):
    rows, seq, width = tokens.shape
    ff = params[-1].shape[0]
    ntask = group_sizes.shape[0]
    full = lambda *shape: pl.BlockSpec(shape, lambda r: (0,) * len(shape), pipeline_mode=pl.Buffered(1))
    const = lambda *shape: pl.BlockSpec(shape, lambda r: (0,) * len(shape))
    act = pl.BlockSpec((1, seq, width), lambda r: (r, 0, 0))
    nar = pl.BlockSpec((1, seq, LANES), lambda r: (r, 0, 0))
    out = lambda shape, dtype: jax.ShapeDtypeStruct(shape, dtype)
    wide = (rows, seq, width)
    any_spec = pl.BlockSpec(memory_space=pl.ANY)
    heads = 2 * PAIRS
    outs = [
        (act, out(wide, bf16)), (act, out(wide, f32)),
        (any_spec, out((width // 2, ff), f32)), (any_spec, out((width // 2, ff), f32)),
        (any_spec, out((ff // 2, width), f32)), (any_spec, out((ff // 2, width), f32)),
        (const(RANK, width), out((RANK, width), f32)), (const(RANK, width), out((RANK, width), f32)),
        (const(8, width), out((8, width), f32)),
        (const(3, 8, width), out((3, 8, width), f32)),
        (const(2, width, LANES), out((2, width, LANES), bf16)), (const(2, LANES, width), out((2, LANES, width), bf16)),
        (const(ntask, params[2].shape[1]), out((ntask, params[2].shape[1]), f32)),
        (const(ntask, params[0].shape[1]), out((ntask, params[0].shape[1]), f32)),
        (act, out(wide, bf16)), (act, out(wide, bf16)), (act, out(wide, bf16)), (act, out(wide, bf16)),
        (act, out(wide, f32)), (act, out(wide, bf16)), (act, out(wide, bf16)), (nar, out((rows, seq, LANES), f32)),
        (act, out(wide, f32)),
        (act, out(wide, bf16)), (act, out(wide, bf16)), (act, out(wide, bf16)), (act, out(wide, bf16)),
        (act, out(wide, f32)), (act, out(wide, bf16)),
        (any_spec, out((rows, heads, seq, seq), bf16)), (any_spec, out((rows, heads, seq, seq), bf16)),
    ]
    return pl.pallas_call(
        functools.partial(forward_kernel, lax.axis_size("dp"), ntask),
        grid=(rows,),
        in_specs=[
            pl.BlockSpec(memory_space=pltpu.SMEM), act, act,
            const(rows, seq), act,
        ] + [full(*item.shape) for item in params],
        out_specs=[spec for spec, _ in outs],
        out_shape=[shape for _, shape in outs],
        scratch_shapes=[
            pltpu.VMEM((64, LANES), f32), pltpu.VMEM((seq, seq), f32), pltpu.VMEM((2, 2, seq, seq), bf16),
            pltpu.SemaphoreType.DMA((2,)), pltpu.VMEM((seq, ff), bf16), pltpu.VMEM((seq, ff), f32),
            pltpu.VMEM((seq, width), f32),
            pltpu.VMEM((width, ff), f32), pltpu.VMEM((ff, width), f32), pltpu.SemaphoreType.DMA((4,)),
        ],
        cost_estimate=SHORT,
        compiler_params=pltpu.CompilerParams(vmem_limit_bytes=60 << 20),
    )(group_sizes, tokens, memory, segments, cotangent, *params)


def attend_back(q_ref, k_ref, v_ref, mixed_ref, share_ref, prob_ref, d_mixed_ref, masked, dq_ref, dk_ref, dv_ref):
    low = low_lanes()
    for pair in range(PAIRS):
        lanes = slice(pair * LANES, (pair + 1) * LANES)
        grad = d_mixed_ref[:, lanes].astype(f32) * share_ref[0, :, lanes]
        product = grad * mixed_ref[0, :, lanes].astype(f32)
        grad = grad.astype(bf16)
        q, k, v = q_ref[0, :, lanes], k_ref[0, :, lanes], v_ref[0, :, lanes]
        zero = jnp.zeros_like(q)
        dq = [None, None]
        whole = [None, None]
        half = [None, None]
        add = lambda old, new: new if old is None else old + new
        for head in range(2):
            own = low if head == 0 else jnp.logical_not(low)
            delta = jnp.sum(jnp.where(own, product, 0.0), axis=-1, keepdims=True)
            head_g, head_q, head_k = (jnp.where(own, item, zero) for item in (grad, q, k))
            for block in range(2):
                rows = slice(block * 256, (block + 1) * 256)
                span = (block + 1) * 256 if masked else 512
                prob = prob_ref[0, pair * 2 + head, rows, :span]
                d_prob = dot_nt(head_g[rows], v[:span])
                d_score = (prob.astype(f32) * (d_prob - delta[rows])).astype(bf16)
                dq[block] = add(dq[block], dot(d_score, head_k[:span]))
                kind = half if span == 256 else whole
                kind[0] = add(kind[0], dot_tn(head_q[rows], d_score))
                kind[1] = add(kind[1], dot_tn(head_g[rows], prob))
        for block in range(2):
            dq_ref[block * 256 : (block + 1) * 256, lanes] = (dq[block] * 0.125).astype(bf16)
        for out_ref, both, first in ((dk_ref, whole[0], half[0]), (dv_ref, whole[1], half[1])):
            if first is None:
                out_ref[:, lanes] = both.T.astype(bf16)
            else:
                out_ref[:256, lanes] = (both[:, :256] + first).T.astype(bf16)
                out_ref[256:, lanes] = both[:, 256:].T.astype(bf16)


def cross_back_kernel(
    grad_two_ref, mixed_ref, q_ref, k_ref, v_ref, share_ref, prob_ref, mem_ref, in_two_ref, after_one_ref,
    narrow_ref, branch_ref, gains_ref, down_w_ref, up_w_ref, cross_qkv_ref, cross_out_ref,
    kept_ref, sent_ref, mem_grad_ref, grad_one_ref, d_branch_ref, up_grad_ref, down_grad_ref, gain_grad_ref,
    d_mixed_ref, dq_ref, dk_ref, dv_ref, total_ref, part_sem,
):
    row = pl.program_id(0)

    @pl.when(row == 0)
    def _():
        for ref in (total_ref, up_grad_ref, down_grad_ref, gain_grad_ref):
            ref[...] = jnp.zeros_like(ref)

    grad_low = grad_two_ref[0].astype(bf16)
    total_ref[0:512] += dot_tn(mixed_ref[0], grad_low)
    d_mixed_ref[...] = dot_nt(grad_low, cross_out_ref[...]).astype(bf16)
    attend_back(q_ref, k_ref, v_ref, mixed_ref, share_ref, prob_ref, d_mixed_ref, False, dq_ref, dk_ref, dv_ref)
    total_ref[512:1024] += dot_tn(in_two_ref[0], dq_ref[...])
    memory_t = mem_ref[0].T
    total_ref[1024:1536] += dot(memory_t, dk_ref[...])
    total_ref[1536:2048] += dot(memory_t, dv_ref[...])

    @pl.when(row == pl.num_programs(0) - 1)
    def _():
        for copy in halves(total_ref, kept_ref, sent_ref, part_sem, 0):
            copy.start()

    mem_grad_ref[0] = dot_nt(dk_ref[...], cross_qkv_ref[1]) + dot_nt(dv_ref[...], cross_qkv_ref[2])
    d_in = dot_nt(dq_ref[...], cross_qkv_ref[0])
    after_one = after_one_ref[0]
    d_after, gain_grad = rms_back(after_one, rms_inv(after_one), gains_ref[1, 0:1], d_in)
    gain_grad_ref[...] += jnp.broadcast_to(gain_grad, gain_grad_ref.shape)
    grad = grad_two_ref[0] + d_after
    grad_one_ref[0] = grad
    grad_low = grad.astype(bf16)
    narrow = narrow_ref[0]
    gate = lax.logistic(narrow)
    narrow_act = (narrow * gate).astype(bf16)
    up_grad_ref[...] += dot_tn(narrow_act, grad_low)[:RANK]
    d_narrow = (dot_nt(grad_low, up_w_ref[0]) * (gate * (1.0 + narrow * (1.0 - gate)))).astype(bf16)
    down_grad_ref[...] += dot_tn(d_narrow, branch_ref[0])[:RANK]
    d_branch_ref[0] = (grad + dot_nt(d_narrow, down_w_ref[0])).astype(bf16)

    @pl.when(row == pl.num_programs(0) - 1)
    def _():
        for copy in halves(total_ref, kept_ref, sent_ref, part_sem, 0):
            copy.wait()


def self_back_kernel(
    d_branch_ref, mixed_ref, q_ref, k_ref, v_ref, share_ref, prob_ref, in_one_ref, x_ref, grad_one_ref, gains_ref,
    self_qkv_ref, self_out_ref,
    kept_ref, sent_ref, input_grad_ref, gain_grad_ref,
    d_mixed_ref, dq_ref, dk_ref, dv_ref, total_ref, part_sem,
):
    row = pl.program_id(0)

    @pl.when(row == 0)
    def _():
        for ref in (total_ref, gain_grad_ref):
            ref[...] = jnp.zeros_like(ref)

    total_ref[0:512] += dot_tn(mixed_ref[0], d_branch_ref[0])
    d_mixed_ref[...] = dot_nt(d_branch_ref[0], self_out_ref[...]).astype(bf16)
    attend_back(q_ref, k_ref, v_ref, mixed_ref, share_ref, prob_ref, d_mixed_ref, True, dq_ref, dk_ref, dv_ref)
    in_one_t = in_one_ref[0].T
    for j, ref in enumerate((dq_ref, dk_ref, dv_ref)):
        total_ref[(1 + j) * 512 : (2 + j) * 512] += dot(in_one_t, ref[...])

    @pl.when(row == pl.num_programs(0) - 1)
    def _():
        for copy in halves(total_ref, kept_ref, sent_ref, part_sem, 0):
            copy.start()

    d_in = None
    for j, ref in enumerate((dq_ref, dk_ref, dv_ref)):
        part = dot_nt(ref[...], self_qkv_ref[j])
        d_in = part if d_in is None else d_in + part
    x = x_ref[0].astype(f32)
    d_x, gain_grad = rms_back(x, rms_inv(x), gains_ref[0, 0:1], d_in)
    gain_grad_ref[...] += jnp.broadcast_to(gain_grad, gain_grad_ref.shape)
    input_grad_ref[0] = grad_one_ref[0] + d_x

    @pl.when(row == pl.num_programs(0) - 1)
    def _():
        for copy in halves(total_ref, kept_ref, sent_ref, part_sem, 0):
            copy.wait()


def small_kernel(
    ntask, sizes_ref, up_one_ref, up_two_ref, down_one_ref, down_two_ref, gain_one_ref, gain_two_ref, gain_three_ref,
    embed_ref, first_ref, second_ref, hgain_ref, hdown_ref, hup_ref, pre_ref,
    kept_ref, sent_ref, out_ref, flat_ref, fold_ref, part_sem,
):
    task, _ = task_place(sizes_ref, ntask, lax.axis_index("dp"))
    _, mine, fold = fold_tables()
    unfold = fold.astype(f32)
    pair_row = lax.broadcasted_iota(jnp.int32, (2 * ntask, LANES), 0)
    task_row = lax.broadcasted_iota(jnp.int32, (ntask, LANES), 0)
    for p, ref in enumerate((down_one_ref, down_two_ref)):
        tall = jnp.concatenate([ref[...], jnp.zeros((LANES - RANK, ref.shape[1]), f32)], axis=0).T
        spread = lax.dot_general(tall, unfold, (((1,), (1,)), ((), ())), precision=highest, preferred_element_type=f32)
        spread = jnp.where(mine, spread, 0.0)
        fold_ref[p] = jnp.sum(spread.reshape(64, 8, LANES), axis=1)
        for a in range(64):
            flat_ref[p : p + 1, a * LANES : (a + 1) * LANES] = fold_ref[p, a : a + 1]
        for a in range(RANK):
            flat_ref[2 + p : 3 + p, a * 512 : (a + 1) * 512] = (up_one_ref, up_two_ref)[p][a : a + 1, :]
    flat_ref[4:8, :] = jnp.zeros((4, flat_ref.shape[1]), f32)
    for a in range(64):
        lanes = slice((a % 4) * LANES, (a % 4 + 1) * LANES)
        r = a // 4
        for base, first_row, second_row in (
            (0, fold_ref[0, a : a + 1], fold_ref[1, a : a + 1]),
            (1024, up_one_ref[r : r + 1, lanes], up_two_ref[r : r + 1, lanes]),
        ):
            block = jnp.where(pair_row == 2 * task, first_row, jnp.where(pair_row == 2 * task + 1, second_row, 0.0))
            out_ref[base + a * 16 : base + (a + 1) * 16, :] = block
    gain = []
    for ref in (gain_one_ref, gain_two_ref, gain_three_ref):
        gain.append(ref[...])
    gain = jnp.concatenate(gain, axis=1)
    for j in range(12):
        block = jnp.where(task_row == task, gain[:, j * LANES : (j + 1) * LANES], 0.0)
        out_ref[2048 + j * 8 : 2056 + j * 8, :] = block
    flat = flat_ref[...]
    down_code = dot_exact_nt(flat, hdown_ref[...])
    up_code = dot_exact_nt(flat, hup_ref[...])
    d_codes = down_code[0:2] + up_code[2:4]
    d_code = d_codes[0:1] + d_codes[1:2] + dot_exact_nt(gain, hgain_ref[...])[0:1]
    one_row = lax.broadcasted_iota(jnp.int32, (8, 1), 0) == 0
    d_code = jnp.where(one_row, jnp.broadcast_to(d_code, (8, d_code.shape[1])), 0.0)
    pre = pick_row(pre_ref[...], task)
    embed = pick_row(embed_ref[...].astype(f32), task)
    hidden = jnp.broadcast_to(pre * lax.logistic(pre), (8, pre.shape[1]))
    exact_tn = lambda left, right: lax.dot_general(
        left, right, (((0,), (0,)), ((), ())), precision=highest, preferred_element_type=f32
    )
    own_second = exact_tn(hidden, d_code)
    d_pre = silu_back(pre, dot_exact(d_code, second_ref[...]))
    own_first = exact_tn(jnp.broadcast_to(embed, (8, embed.shape[1])), d_pre)
    own_task = dot_exact_nt(d_pre, first_ref[...])[0:1]
    rows = lax.broadcasted_iota(jnp.int32, (8, own_task.shape[1]), 0)
    task_block = jnp.where(rows == task, own_task, 0.0)
    code_block = jnp.where(rows == 0, d_codes[0:1], jnp.where(rows == 1, d_codes[1:2], 0.0))
    out_ref[2144:2208, :] = own_first
    out_ref[2208:2336, :] = jnp.concatenate([own_second, jnp.zeros_like(own_second)], axis=1)
    out_ref[2336:2344, :] = jnp.concatenate([task_block, code_block], axis=1)
    out_ref[2344:, :] = jnp.zeros((out_ref.shape[0] - 2344, LANES), f32)
    copies = halves(out_ref, kept_ref, sent_ref, part_sem, 0)
    for copy in copies:
        copy.start()
    for copy in copies:
        copy.wait()


def spread_kernel(
    ntask, sum_ref, code_ref, position_ref,
    task_ref, pos_ref, first_ref, second_ref, gain_ref, down_ref, up_ref,
):
    code = code_ref[...]
    emb = code.shape[1]
    position = position_ref[...].astype(f32)
    codes = jnp.stack([code + position[0:1], code + position[1:2]], axis=1).reshape(2 * ntask, emb)
    exact_tn = lambda left, right: lax.dot_general(
        left, right, (((0,), (0,)), ((), ())), precision=highest, preferred_element_type=f32
    )
    wide = lambda base, count, step: jnp.concatenate(
        [sum_ref[base + a * step : base + (a + 1) * step, :] for a in range(count)], axis=1
    )
    down_ref[...] = exact_tn(codes, wide(0, 64, 16))
    up_ref[...] = exact_tn(codes, wide(1024, 64, 16))
    gain_ref[...] = exact_tn(code, wide(2048, 12, 8))
    first_ref[...] = sum_ref[2144:2208, :]
    second_ref[...] = sum_ref[2208:2336, :emb]
    task_ref[...] = sum_ref[2336:2344, :emb]
    pos_ref[...] = sum_ref[2336:2338, emb:]


def call_rows(kernel, rows, ins, outs, scratch, limit=60):
    def spec(item, blocked):
        if blocked is None:
            return pl.BlockSpec(memory_space=pl.ANY)
        shape = item.shape
        if blocked:
            return pl.BlockSpec((1,) + tuple(shape[1:]), lambda r: (r,) + (0,) * (len(shape) - 1))
        return pl.BlockSpec(tuple(shape), lambda r: (0,) * len(shape))

    return pl.pallas_call(
        kernel,
        grid=(rows,),
        in_specs=[spec(*item) for item in ins],
        out_specs=[spec(*item) for item in outs],
        out_shape=[item for item, _ in outs],
        scratch_shapes=scratch,
        cost_estimate=SHORT,
        compiler_params=pltpu.CompilerParams(vmem_limit_bytes=limit << 20),
    )(*[item for item, _ in ins])


def add_kernel(bits, kept_ref, got_ref, sent_ref, next_ref):
    half = sent_ref.shape[0]
    side = upper(lax.axis_index("dp"), bits)
    theirs = pl.ds(pl.multiple_of((1 - side) * half, half), half)
    mine = pl.ds(pl.multiple_of(side * half, half), half)
    sent_ref[...] = kept_ref[theirs] + got_ref[theirs]
    next_ref[...] = kept_ref[mine] + got_ref[mine]


def join_kernel(bits, cuts, own_ref, got_ref, *refs):
    *out_refs, sem = refs
    half = own_ref.shape[0]
    side = upper(lax.axis_index("dp"), bits)

    def copies(low_ref, high_ref):
        found, at = [], 0
        for cut, out_ref in zip(cuts, out_refs):
            for source, first in ((low_ref, 0), (high_ref, half)):
                low, high = max(at, first), min(at + cut, first + half)
                if low < high:
                    found.append((source.at[pl.ds(low - first, high - low)], out_ref.at[pl.ds(low - at, high - low)]))
            at += cut
        return [pltpu.make_async_copy(*pair, sem.at[i]) for i, pair in enumerate(found)]

    for place, refs in ((0, (own_ref, got_ref)), (1, (got_ref, own_ref))):

        @pl.when(side == place)
        def _():
            every = copies(*refs)
            for copy in every:
                copy.start()
            for copy in every:
                copy.wait()


def add_parts(kept, got, bits):
    half = jax.ShapeDtypeStruct((kept.shape[0] // 2,) + kept.shape[1:], f32)
    return pl.pallas_call(
        functools.partial(add_kernel, bits),
        out_shape=[half, half],
        cost_estimate=SHORT,
        compiler_params=pltpu.CompilerParams(vmem_limit_bytes=16 << 20),
    )(kept, got)


def join_parts(own, got, bits, cuts):
    any_spec = pl.BlockSpec(memory_space=pl.ANY)
    return pl.pallas_call(
        functools.partial(join_kernel, bits, cuts),
        in_specs=[any_spec] * 2,
        out_specs=[any_spec] * len(cuts),
        out_shape=[jax.ShapeDtypeStruct((cut,) + own.shape[1:], f32) for cut in cuts],
        scratch_shapes=[pltpu.SemaphoreType.DMA((2 + len(cuts),))],
        cost_estimate=SHORT,
        compiler_params=pltpu.CompilerParams(vmem_limit_bytes=1 << 20),
    )(own, got)


SEQUENCE = "01A012B0213C03442013014203410234102013243142134223434D"
ORDER = ((1, 1), (2, 4), (4, 2), (8, 8), (16, 16))


class Line:
    def __init__(self):
        self.last = None

    def tie(self, values):
        if self.last is None:
            return values
        values, self.last["kept"] = lax.optimization_barrier((values, self.last["kept"]))
        return values


def summing(kept, sent, cuts, line, found):
    devices = lax.axis_size("dp")
    state = {}

    def swap(values, bits):
        moves = [(i, i ^ bits[i % 2]) for i in range(devices)]
        return lax.ppermute(values, "dp", moves)

    def mark(value):
        state["kept"] = value
        line.last = state

    high = [(32 << i, 32 << i) for i in range(max(devices // 32, 1).bit_length() - 1)]
    sent = line.tie(sent)
    got = swap(sent, ORDER[0])
    mark(kept)
    yield
    for bits in ORDER[1:-1]:
        got = line.tie(got)
        sent, kept = add_parts(state["kept"], got, bits)
        got = swap(sent, bits)
        mark(kept)
        yield
    for bits in list(ORDER[-1:]) + high:
        got = line.tie(got)
        total = state["kept"] + got
        got = swap(total, bits)
        mark(total)
        yield
    got = line.tie(got)
    total = state["kept"] + got
    for bits in ORDER[:-1][::-1]:
        got = swap(total, bits)
        mark(total)
        yield
        got = line.tie(got)
        own = state["kept"]
        if bits == ORDER[0]:
            break
        (total,) = join_parts(own, got, bits, (2 * own.shape[0],))
    parts = join_parts(own, got, ORDER[0], cuts)
    mark(parts[-1])
    found.append((parts[:-1], state))


def on_device(
    tokens, memory, segments, cotangent, group_sizes, task_embed, position_embed, hyper_first, hyper_second,
    hyper_gain, hyper_down, hyper_up, self_qkv, self_out, cross_qkv, cross_out, ffn_in, ffn_out,
):
    rows, seq, width = tokens.shape
    ntask = group_sizes.shape[0]
    hyper_second_t = hyper_second.T
    params = (
        task_embed, position_embed, hyper_first, hyper_second_t, hyper_gain, hyper_down, hyper_up,
        self_qkv, self_out, cross_qkv, cross_out, ffn_in, ffn_out,
    )
    (
        output, grad_two, in_kept, in_sent, out_kept, out_sent, up_two, down_two, gain_three,
        gains, down_w, up_w, pre, code,
        in_one, q_one, k_one, v_one, share_one, mixed_one, branch, narrow, after_one,
        in_two, q_two, k_two, v_two, share_two, mixed_two, prob_one, prob_two,
    ) = run_forward(tokens, memory, segments, cotangent, group_sizes, params)
    like = lambda shape, dtype=f32: jax.ShapeDtypeStruct(shape, dtype)
    wide = tokens.shape
    row_scratch = [pltpu.VMEM((seq, width), bf16)] * 4
    row_scratch += [pltpu.VMEM((4 * width, width), f32), pltpu.SemaphoreType.DMA((2,))]
    pair = (2 * width, width)
    line = Line()
    sums = [[] for _ in range(5)]
    ff = ffn_out.shape[0]

    def start(which, kept, sent, cuts):
        return summing(kept, sent, cuts, line, sums[which])

    def mark(value):
        line.last = {"kept": value}
        return line.last

    chunks = {"0": start(0, out_kept, out_sent, (ff,)), "1": start(1, in_kept, in_sent, (width,))}
    for step in SEQUENCE:
        if step in chunks:
            next(chunks[step], None)
        elif step == "A":
            grad_two = line.tie(grad_two)
            cross_kept, cross_sent, memory_grad, grad_one, d_branch, up_one, down_one, gain_two = call_rows(
                cross_back_kernel,
                rows,
                [
                    (grad_two, True), (mixed_two, True), (q_two, True), (k_two, True), (v_two, True), (share_two, True),
                    (prob_two, True), (memory, True), (in_two, True), (after_one, True), (narrow, True), (branch, True),
                    (gains, False), (down_w, False), (up_w, False), (cross_qkv, False), (cross_out, False),
                ],
                [
                    (like(pair), None), (like(pair), None), (like(wide), True), (like(wide), True),
                    (like(wide, bf16), True), (like((RANK, width)), False), (like((RANK, width)), False), (like((8, width)), False),
                ],
                row_scratch,
            )
            memory_grad = mark(memory_grad)
            chunks["2"] = start(2, cross_kept, cross_sent, (width, 3 * width))
        elif step == "B":
            d_branch = line.tie(d_branch)
            self_kept, self_sent, input_grad, gain_one = call_rows(
                self_back_kernel,
                rows,
                [
                    (d_branch, True), (mixed_one, True), (q_one, True), (k_one, True), (v_one, True), (share_one, True),
                    (prob_one, True), (in_one, True), (tokens, True), (grad_one, True), (gains, False),
                    (self_qkv, False), (self_out, False),
                ],
                [(like(pair), None), (like(pair), None), (like(wide), True), (like((8, width)), False)],
                row_scratch,
            )
            input_grad = mark(input_grad)
            chunks["3"] = start(3, self_kept, self_sent, (width, 3 * width))
        elif step == "C":
            gain_one = line.tie(gain_one)
            small_kept, small_sent = pl.pallas_call(
                functools.partial(small_kernel, ntask),
                out_shape=[like((1280, LANES))] * 2,
                in_specs=[pl.BlockSpec(memory_space=pltpu.SMEM)] + [pl.BlockSpec(memory_space=pltpu.VMEM)] * 14,
                out_specs=[pl.BlockSpec(memory_space=pl.ANY)] * 2,
                scratch_shapes=[
                    pltpu.VMEM((2560, LANES), f32), pltpu.VMEM((8, 8192), f32), pltpu.VMEM((2, 64, LANES), f32),
                    pltpu.SemaphoreType.DMA((2,)),
                ],
                cost_estimate=SHORT,
        compiler_params=pltpu.CompilerParams(vmem_limit_bytes=32 << 20),
            )(
                group_sizes, up_one, up_two, down_one, down_two, gain_one, gain_two, gain_three,
                task_embed, hyper_first, hyper_second_t, hyper_gain, hyper_down, hyper_up, pre,
            )
            mark(small_kept)
            chunks["4"] = start(4, small_kept, small_sent, (2560,))
        else:
            for _ in chunks["4"]:
                pass
            sum_small = line.tie(sums[4][0][1]["kept"])
            task_grad, position_grad, first_grad, second_grad, gain_grad, down_grad, up_grad = pl.pallas_call(
                functools.partial(spread_kernel, ntask),
                out_shape=[
                    like(item.shape)
                    for item in (task_embed, position_embed, hyper_first, hyper_second, hyper_gain, hyper_down, hyper_up)
                ],
                cost_estimate=SHORT,
        compiler_params=pltpu.CompilerParams(vmem_limit_bytes=32 << 20),
            )(sum_small, code, position_embed)
            task_grad = mark(task_grad)
    for rest in chunks.values():
        for _ in rest:
            pass
    memory_grad, input_grad, task_grad = memory_grad["kept"], input_grad["kept"], task_grad["kept"]
    sum_out, sum_in, cross_qkv_grad, self_qkv_grad = (sums[i][0][1]["kept"] for i in range(4))
    cross_out_grad, self_out_grad = sums[2][0][0][0], sums[3][0][0][0]
    cross_qkv_grad = cross_qkv_grad.reshape(cross_qkv.shape)
    self_qkv_grad = self_qkv_grad.reshape(self_qkv.shape)
    return (
        output, input_grad, memory_grad, task_grad, position_grad, first_grad, second_grad, gain_grad, down_grad,
        up_grad, self_qkv_grad, self_out_grad, cross_qkv_grad, cross_out_grad, sum_in, sum_out,
    )


def solution(mesh):
    split = P("dp", None, None)
    return jax.shard_map(
        on_device,
        mesh=mesh,
        in_specs=(split, split, P("dp", None), split) + (P(),) * 14,
        out_specs=(split,) * 3 + (P(),) * 13,
        check_vma=False,
    )
```

profile of v0, /device:TPU:0, one launch (start us, length us, event | category | flops | bytes accessed | tf_op | source)
XLA Modules:
  0.0 316.5 jit_solution(8410446259748228421)
XLA Ops:
  0.6 57.2 %shard_map.297 = (bf16[2,512,512]{2,1,0:T(8,128)(2,1)}, f32[2,512,512]{2,1,0:T(8,128)}, f32[256,2048]{1,0:T(8,128)}, f32[256,2048]{1,0:T(8,128)}, f32[1024,512]{...) custom-call(s32[8]{0:T(128)} %sizes_ref.3, ...), custom_call_target="tpu_custom_call" | custom-call | flops 1 | bytes 1 | tf_op jit(solution)/shard_map/pallas_call | solution.py:345
  58.5 25.8 %shard_map.298 = (f32[1024,512]{1,0:T(8,128)}, f32[1024,512]{1,0:T(8,128)}, f32[2,512,512]{2,1,0:T(8,128)}, f32[2,512,512]{2,1,0:T(8,128)}, bf16[2,512,512]{2,1,...) custom-call(f32[2,512,512]{2,1,0:T(8,128)} %get-tuple-element.212.grad_two_ref, ...), custom_call_target="tpu_custom_call" | custom-call | flops 1 | bytes 1 | tf_op jit(solution)/shard_map/pallas_call | solution.py:590
  84.3 2.9 shard_map.299
  87.2 3.2 shard_map.301
  90.8 2.6 collective-permute-start.1
  93.4 19.0 %shard_map.300 = (f32[1024,512]{1,0:T(8,128)}, f32[1024,512]{1,0:T(8,128)}, f32[2,512,512]{2,1,0:T(8,128)}, f32[8,512]{1,0:T(8,128)}) custom-call(bf16[2,512,512]{2,1,0:T(8,128)(2,1)} %get-tuple-element.231.d_branch_ref, bf16[2,512,512]{2,1,0:T(8,128)(2,1)} %get-tuple-element.232.mixed_ref, bf16[2,512,512]{2,1,0:T(8,128)(2,1)} %get-tuple-element.233.q_ref, ...), custom_call_target="tpu_custom_call" | custom-call | flops 1 | bytes 1 | tf_op jit(solution)/shard_map/pallas_call | solution.py:590
  122.9 5.0 %shard_map.304 = (f32[1280,128]{1,0:T(8,128)S(1)}, f32[1280,128]{1,0:T(8,128)S(1)}) custom-call(s32[8]{0:T(128)S(1)} %copy-done.21, f32[16,512]{1,0:T(8,128)S(1)} %copy-done.13, f32[16,512]{1,0:T(8,128)S(1)} %copy-done.11, f32[16,512]{1,0:T(8,128)S(1)} %copy-done.14, f32[16,512]{1,0:T(8,128)S(1)} %copy-done.12, f32[8,512]{1,0:T(8,128)S(1)} %copy-done.17, ...), custom_call_target="tpu_custom_call" | custom-call | flops 1 | bytes 1 | tf_op jit(solution)/shard_map/pallas_call | solution.py:792
  127.9 5.0 %collective-permute-done.7.got_ref = f32[256,512]{1,0:T(8,128)S(1)} collective-permute-done((f32[256,512]{1,0:T(8,128)S(1)}, f32[256,512]{1,0:T(8,128)S(1)}, u32[]{:S(2)}, u32[]{:S(2)}) %collective-permute-start.7) | collective-permute-done | bytes 524320 | tf_op jit(solution)/shard_map/ppermute | solution.py:681
  133.2 3.1 collective-permute-start.11
  140.1 5.0 %collective-permute-done.13 = f32[128,512]{1,0:T(8,128)S(1)} collective-permute-done((f32[128,512]{1,0:T(8,128)S(1)}, f32[128,512]{1,0:T(8,128)S(1)}, u32[]{:S(2)}, u32[]{:S(2)}) %collective-permute-start.13) | collective-permute-done | bytes 262176 | tf_op jit(solution)/shard_map/ppermute | solution.py:681
  145.1 2.7 collective-permute-start.15
  153.0 8.7 %collective-permute-done.11.got_ref = f32[512,512]{1,0:T(8,128)S(1)} collective-permute-done((f32[512,512]{1,0:T(8,128)S(1)}, f32[512,512]{1,0:T(8,128)S(1)}, u32[]{:S(2)}, u32[]{:S(2)}) %collective-permute-start.11) | collective-permute-done | bytes 1048608 | tf_op jit(solution)/shard_map/ppermute | solution.py:681
  165.6 5.3 %collective-permute-done.18.got_ref = f32[128,512]{1,0:T(8,128)S(1)} collective-permute-done((f32[128,512]{1,0:T(8,128)S(1)}, f32[128,512]{1,0:T(8,128)S(1)}, u32[]{:S(2)}, u32[]{:S(2)}) %collective-permute-start.18) | collective-permute-done | bytes 262176 | tf_op jit(solution)/shard_map/ppermute | solution.py:681
  172.8 2.7 collective-permute-start.23
  176.0 6.0 %collective-permute-done.16.got_ref = f32[320,128]{1,0:T(8,128)S(1)} collective-permute-done((f32[320,128]{1,0:T(8,128)S(1)}, f32[320,128]{1,0:T(8,128)S(1)}, u32[]{:S(2)}, u32[]{:S(2)}) %collective-permute-start.16) | collective-permute-done | bytes 163872 | tf_op jit(solution)/shard_map/ppermute | solution.py:681
  182.0 4.5 %collective-permute-done.23 = f32[32,2048]{1,0:T(8,128)S(1)} collective-permute-done((f32[32,2048]{1,0:T(8,128)S(1)}, f32[32,2048]{1,0:T(8,128)S(1)}, u32[]{:S(2)}, u32[]{:S(2)}) %collective-permute-start.23) | collective-permute-done | bytes 262176 | tf_op jit(solution)/shard_map/ppermute | solution.py:681
  191.9 5.2 %collective-permute-done.21 = f32[128,512]{1,0:T(8,128)S(1)} collective-permute-done((f32[128,512]{1,0:T(8,128)S(1)}, f32[128,512]{1,0:T(8,128)S(1)}, u32[]{:S(2)}, u32[]{:S(2)}) %collective-permute-start.21) | collective-permute-done | bytes 262176 | tf_op jit(solution)/shard_map/ppermute | solution.py:681
  197.1 5.6 %collective-permute-done.20 = f32[128,512]{1,0:T(8,128)S(1)} collective-permute-done((f32[128,512]{1,0:T(8,128)S(1)}, f32[128,512]{1,0:T(8,128)S(1)}, u32[]{:S(2)}, u32[]{:S(2)}) %collective-permute-start.20) | collective-permute-done | bytes 262176 | tf_op jit(solution)/shard_map/ppermute | solution.py:681
  202.7 5.9 %collective-permute-done.19 = f32[160,128]{1,0:T(8,128)S(1)} collective-permute-done((f32[160,128]{1,0:T(8,128)S(1)}, f32[160,128]{1,0:T(8,128)S(1)}, u32[]{:S(2)}, u32[]{:S(2)}) %collective-permute-start.19) | collective-permute-done | bytes 81952 | tf_op jit(solution)/shard_map/ppermute | solution.py:681
  209.7 3.1 collective-permute-start.28
  212.8 12.8 %collective-permute-done.28 = f32[128,512]{1,0:T(8,128)S(1)} collective-permute-done((f32[128,512]{1,0:T(8,128)S(1)}, f32[128,512]{1,0:T(8,128)S(1)}, u32[]{:S(2)}, u32[]{:S(2)}) %collective-permute-start.28) | collective-permute-done | bytes 262176 | tf_op jit(solution)/shard_map/ppermute | solution.py:681
  228.8 4.1 %collective-permute-start.32 = (f32[128,512]{1,0:T(8,128)S(1)}, f32[128,512]{1,0:T(8,128)S(1)}, u32[]{:S(2)}, u32[]{:S(2)}) collective-permute-start(f32[128,512]{1,0:T(8,128)S(1)} %add.37.own_ref), channel_id=1, source_target_pairs={{0,8},{1,9},{2,10},{3,11},{4,12},{5,13},{6,14},{7,15},{8,0},{9,1},... | collective-permute-start | bytes 786440 | tf_op jit(solution)/shard_map/ppermute | solution.py:681
  232.9 9.9 %collective-permute-done.24 = f32[128,512]{1,0:T(8,128)S(1)} collective-permute-done((f32[128,512]{1,0:T(8,128)S(1)}, f32[128,512]{1,0:T(8,128)S(1)}, u32[]{:S(2)}, u32[]{:S(2)}) %collective-permute-start.24) | collective-permute-done | bytes 262176 | tf_op jit(solution)/shard_map/ppermute | solution.py:681
  244.8 4.9 %collective-permute-done.31 = f32[160,128]{1,0:T(8,128)S(1)} collective-permute-done((f32[160,128]{1,0:T(8,128)S(1)}, f32[160,128]{1,0:T(8,128)S(1)}, u32[]{:S(2)}, u32[]{:S(2)}) %collective-permute-start.31) | collective-permute-done | bytes 81952 | tf_op jit(solution)/shard_map/ppermute | solution.py:681
  255.1 3.9 %collective-permute-done.33.got_ref = f32[160,128]{1,0:T(8,128)S(1)} collective-permute-done((f32[160,128]{1,0:T(8,128)S(1)}, f32[160,128]{1,0:T(8,128)S(1)}, u32[]{:S(2)}, u32[]{:S(2)}) %collective-permute-start.33) | collective-permute-done | bytes 81952 | tf_op jit(solution)/shard_map/ppermute | solution.py:681
  266.7 10.8 %collective-permute-done.36.got_ref = f32[256,512]{1,0:T(8,128)S(1)} collective-permute-done((f32[256,512]{1,0:T(8,128)S(1)}, f32[256,512]{1,0:T(8,128)S(1)}, u32[]{:S(2)}, u32[]{:S(2)}) %collective-permute-start.36) | collective-permute-done | bytes 524320 | tf_op jit(solution)/shard_map/ppermute | solution.py:681
  277.6 3.4 %collective-permute-done.35.got_ref = f32[320,128]{1,0:T(8,128)S(1)} collective-permute-done((f32[320,128]{1,0:T(8,128)S(1)}, f32[320,128]{1,0:T(8,128)S(1)}, u32[]{:S(2)}, u32[]{:S(2)}) %collective-permute-start.35) | collective-permute-done | bytes 163872 | tf_op jit(solution)/shard_map/ppermute | solution.py:681
  281.4 2.6 collective-permute-done.40.got_ref
  285.1 3.4 %collective-permute-done.41.got_ref = f32[1024,512]{1,0:T(8,128)S(1)} collective-permute-done((f32[1024,512]{1,0:T(8,128)S(1)}, f32[1024,512]{1,0:T(8,128)S(1)}, u32[]{:S(2)}, u32[]{:S(2)}) %collective-permute-start.41) | collective-permute-done | bytes 2097184 | tf_op jit(solution)/shard_map/ppermute | solution.py:681
  290.5 8.7 %collective-permute-done.39.got_ref = f32[512,512]{1,0:T(8,128)S(1)} collective-permute-done((f32[512,512]{1,0:T(8,128)S(1)}, f32[512,512]{1,0:T(8,128)S(1)}, u32[]{:S(2)}, u32[]{:S(2)}) %collective-permute-start.39) | collective-permute-done | bytes 1048608 | tf_op jit(solution)/shard_map/ppermute | solution.py:681
  300.2 6.4 %collective-permute-done.43.got_ref = f32[640,128]{1,0:T(8,128)S(1)} collective-permute-done((f32[640,128]{1,0:T(8,128)S(1)}, f32[640,128]{1,0:T(8,128)S(1)}, u32[]{:S(2)}, u32[]{:S(2)}) %collective-permute-start.43) | collective-permute-done | bytes 327712 | tf_op jit(solution)/shard_map/ppermute | solution.py:681
  309.7 5.8 %shard_map.336 = (f32[8,64]{1,0:T(8,128)}, f32[2,64]{1,0:T(2,128)}, f32[64,128]{1,0:T(8,128)}, f32[128,64]{1,0:T(8,128)S(1)}, f32[64,1536]{1,0:T(8,128)}, /*index=5*/f32[64,8192]{1,0:T(8,128)}, f32[64,8192]{1,0:T(8,128)}) custom-call(f32[2560,128]{1,0:T(8,128)S(1)} %shard_map.335.sum_ref, f32[8,64]{1,0:T(8,128)S(1)} %copy-done.19, bf16[2,64]{1,0:T(2,128)(2,1)S(1)} %copy-done.22), custom_call_target="tpu_custom_call" | custom-call | flops 1 | bytes 1 | tf_op jit(solution)/shard_map/pallas_call | solution.py:813
  (157 shorter events, 59.8 us)
Async XLA Ops:
  57.9 26.4 %collective-permute-start = (f32[1024,512]{1,0:T(8,128)}, f32[1024,512]{1,0:T(8,128)}, u32[]{:S(2)}, u32[]{:S(2)}) collective-permute-start(f32[1024,512]{1,0:T(8,128)} %get-tuple-element.209), channel_id=1, source_target_pairs={{0,1},{1,0},{2,3},{3,2},{4,5},{5,4},{6,7},{7,6},{8,9},{9,8},{10,11... | collective-permute-start | bytes 6291464 | tf_op jit(solution)/shard_map/ppermute | solution.py:681
  58.4 28.8 %collective-permute-start.2 = (f32[256,2048]{1,0:T(8,128)}, f32[256,2048]{1,0:T(8,128)}, u32[]{:S(2)}, u32[]{:S(2)}) collective-permute-start(f32[256,2048]{1,0:T(8,128)} %get-tuple-element.244), channel_id=1, source_target_pairs={{0,1},{1,0},{2,3},{3,2},{4,5},{5,4},{6,7},{7,6},{8,9},{9,8},{10,11... | collective-permute-start | bytes 6291464 | tf_op jit(solution)/shard_map/ppermute | solution.py:681
  90.4 24.7 %collective-permute-start.4 = (f32[1024,512]{1,0:T(8,128)}, f32[1024,512]{1,0:T(8,128)S(1)}, u32[]{:S(2)}, u32[]{:S(2)}) collective-permute-start(f32[1024,512]{1,0:T(8,128)} %get-tuple-element.251), channel_id=1, source_target_pairs={{0,1},{1,0},{2,3},{3,2},{4,5},{5,4},{6,7},{7,6},{8,9},{9,8},{10,11... | collective-permute-start | bytes 6291464 | tf_op jit(solution)/shard_map/ppermute | solution.py:681
  90.8 21.6 %collective-permute-start.1 = (f32[512,512]{1,0:T(8,128)}, f32[512,512]{1,0:T(8,128)}, u32[]{:S(2)}, u32[]{:S(2)}) collective-permute-start(f32[512,512]{1,0:T(8,128)} %get-tuple-element.228), channel_id=1, source_target_pairs={{0,2},{1,5},{2,0},{3,7},{4,6},{5,1},{6,4},{7,3},{8,10},{9,13},{10,... | collective-permute-start | bytes 3145736 | tf_op jit(solution)/shard_map/ppermute | solution.py:681
  93.4 24.3 %collective-permute-start.3 = (f32[128,2048]{1,0:T(8,128)}, f32[128,2048]{1,0:T(8,128)}, u32[]{:S(2)}, u32[]{:S(2)}) collective-permute-start(f32[128,2048]{1,0:T(8,128)} %get-tuple-element.247), channel_id=1, source_target_pairs={{0,2},{1,5},{2,0},{3,7},{4,6},{5,1},{6,4},{7,3},{8,10},{9,13},{10,... | collective-permute-start | bytes 3145736 | tf_op jit(solution)/shard_map/ppermute | solution.py:681
  119.1 13.9 %collective-permute-start.6 = (f32[1024,512]{1,0:T(8,128)S(1)}, f32[1024,512]{1,0:T(8,128)S(1)}, u32[]{:S(2)}, u32[]{:S(2)}) collective-permute-start(f32[1024,512]{1,0:T(8,128)S(1)} %copy-done.23), channel_id=1, source_target_pairs={{0,1},{1,0},{2,3},{3,2},{4,5},{5,4},{6,7},{7,6},{8,9},{9,8},{10,11... | collective-permute-start | bytes 6291464 | tf_op jit(solution)/shard_map/ppermute | solution.py:681
  119.2 13.8 %collective-permute-start.7 = (f32[256,512]{1,0:T(8,128)S(1)}, f32[256,512]{1,0:T(8,128)S(1)}, u32[]{:S(2)}, u32[]{:S(2)}) collective-permute-start(f32[256,512]{1,0:T(8,128)S(1)} %get-tuple-element.277), channel_id=1, source_target_pairs={{0,4},{1,3},{2,6},{3,1},{4,0},{5,7},{6,2},{7,5},{8,12},{9,11},{10,... | collective-permute-start | bytes 1572872 | tf_op jit(solution)/shard_map/ppermute | solution.py:681
  121.2 18.7 %collective-permute-start.5 = (f32[512,512]{1,0:T(8,128)S(1)}, f32[512,512]{1,0:T(8,128)S(1)}, u32[]{:S(2)}, u32[]{:S(2)}) collective-permute-start(f32[512,512]{1,0:T(8,128)S(1)} %get-tuple-element.258), channel_id=1, source_target_pairs={{0,2},{1,5},{2,0},{3,7},{4,6},{5,1},{6,4},{7,3},{8,10},{9,13},{10,... | collective-permute-start | bytes 3145736 | tf_op jit(solution)/shard_map/ppermute | solution.py:681
  133.2 28.5 %collective-permute-start.11 = (f32[512,512]{1,0:T(8,128)S(1)}, f32[512,512]{1,0:T(8,128)S(1)}, u32[]{:S(2)}, u32[]{:S(2)}) collective-permute-start(f32[512,512]{1,0:T(8,128)S(1)} %get-tuple-element.291), channel_id=1, source_target_pairs={{0,2},{1,5},{2,0},{3,7},{4,6},{5,1},{6,4},{7,3},{8,10},{9,13},{10,... | collective-permute-start | bytes 3145736 | tf_op jit(solution)/shard_map/ppermute | solution.py:681
  136.4 14.9 %collective-permute-start.12 = (f32[64,2048]{1,0:T(8,128)S(1)}, f32[64,2048]{1,0:T(8,128)S(1)}, u32[]{:S(2)}, u32[]{:S(2)}) collective-permute-start(f32[64,2048]{1,0:T(8,128)S(1)} %get-tuple-element.293), channel_id=1, source_target_pairs={{0,4},{1,3},{2,6},{3,1},{4,0},{5,7},{6,2},{7,5},{8,12},{9,11},{10,... | collective-permute-start | bytes 1572872 | tf_op jit(solution)/shard_map/ppermute | solution.py:681
  145.1 16.7 %collective-permute-start.15 = (f32[128,512]{1,0:T(8,128)S(1)}, f32[128,512]{1,0:T(8,128)S(1)}, u32[]{:S(2)}, u32[]{:S(2)}) collective-permute-start(f32[128,512]{1,0:T(8,128)S(1)} %add.30), channel_id=1, source_target_pairs={{0,16},{1,17},{2,18},{3,19},{4,20},{5,21},{6,22},{7,23},{8,24},{9,... | collective-permute-start | bytes 786440 | tf_op jit(solution)/shard_map/ppermute | solution.py:681
  147.8 17.7 %collective-permute-start.9 = (f32[256,512]{1,0:T(8,128)S(1)}, f32[256,512]{1,0:T(8,128)S(1)}, u32[]{:S(2)}, u32[]{:S(2)}) collective-permute-start(f32[256,512]{1,0:T(8,128)S(1)} %get-tuple-element.288), channel_id=1, source_target_pairs={{0,4},{1,3},{2,6},{3,1},{4,0},{5,7},{6,2},{7,5},{8,12},{9,11},{10,... | collective-permute-start | bytes 1572872 | tf_op jit(solution)/shard_map/ppermute | solution.py:681
  149.4 16.1 %collective-permute-start.10 = (f32[640,128]{1,0:T(8,128)S(1)}, f32[640,128]{1,0:T(8,128)S(1)}, u32[]{:S(2)}, u32[]{:S(2)}) collective-permute-start(f32[640,128]{1,0:T(8,128)S(1)} %get-tuple-element.290), channel_id=1, source_target_pairs={{0,2},{1,5},{2,0},{3,7},{4,6},{5,1},{6,4},{7,3},{8,10},{9,13},{10,... | collective-permute-start | bytes 983048 | tf_op jit(solution)/shard_map/ppermute | solution.py:681
  151.3 12.6 %collective-permute-start.14 = (f32[32,2048]{1,0:T(8,128)S(1)}, f32[32,2048]{1,0:T(8,128)S(1)}, u32[]{:S(2)}, u32[]{:S(2)}) collective-permute-start(f32[32,2048]{1,0:T(8,128)S(1)} %get-tuple-element.301), channel_id=1, source_target_pairs={{0,8},{1,9},{2,10},{3,11},{4,12},{5,13},{6,14},{7,15},{8,0},{9,1},... | collective-permute-start | bytes 786440 | tf_op jit(solution)/shard_map/ppermute | solution.py:681
  163.9 12.1 %collective-permute-start.17 = (f32[256,512]{1,0:T(8,128)S(1)}, f32[256,512]{1,0:T(8,128)S(1)}, u32[]{:S(2)}, u32[]{:S(2)}) collective-permute-start(f32[256,512]{1,0:T(8,128)S(1)} %get-tuple-element.313), channel_id=1, source_target_pairs={{0,4},{1,3},{2,6},{3,1},{4,0},{5,7},{6,2},{7,5},{8,12},{9,11},{10,... | collective-permute-start | bytes 1572872 | tf_op jit(solution)/shard_map/ppermute | solution.py:681
  171.0 15.5 %collective-permute-start.22 = (f32[256,512]{1,0:T(8,128)S(1)}, f32[256,512]{1,0:T(8,128)S(1)}, u32[]{:S(2)}, u32[]{:S(2)}) collective-permute-start(f32[256,512]{1,0:T(8,128)S(1)} %shard_map.314.own_ref), channel_id=1, source_target_pairs={{0,4},{1,3},{2,6},{3,1},{4,0},{5,7},{6,2},{7,5},{8,12},{9,11},{10,... | collective-permute-start | bytes 1572872 | tf_op jit(solution)/shard_map/ppermute | solution.py:681
  172.8 13.7 %collective-permute-start.23 = (f32[32,2048]{1,0:T(8,128)S(1)}, f32[32,2048]{1,0:T(8,128)S(1)}, u32[]{:S(2)}, u32[]{:S(2)}) collective-permute-start(f32[32,2048]{1,0:T(8,128)S(1)} %add.32), channel_id=1, source_target_pairs={{0,16},{1,17},{2,18},{3,19},{4,20},{5,21},{6,22},{7,23},{8,24},{9,... | collective-permute-start | bytes 786440 | tf_op jit(solution)/shard_map/ppermute | solution.py:681
  186.7 22.3 %collective-permute-start.25 = (f32[512,512]{1,0:T(8,128)S(1)}, f32[512,512]{1,0:T(8,128)S(1)}, u32[]{:S(2)}, u32[]{:S(2)}) collective-permute-start(f32[512,512]{1,0:T(8,128)S(1)} %shard_map.317.own_ref), channel_id=1, source_target_pairs={{0,2},{1,5},{2,0},{3,7},{4,6},{5,1},{6,4},{7,3},{8,10},{9,13},{10,... | collective-permute-start | bytes 3145736 | tf_op jit(solution)/shard_map/ppermute | solution.py:681
  188.5 14.1 %collective-permute-start.20 = (f32[128,512]{1,0:T(8,128)S(1)}, f32[128,512]{1,0:T(8,128)S(1)}, u32[]{:S(2)}, u32[]{:S(2)}) collective-permute-start(f32[128,512]{1,0:T(8,128)S(1)} %get-tuple-element.324), channel_id=1, source_target_pairs={{0,8},{1,9},{2,10},{3,11},{4,12},{5,13},{6,14},{7,15},{8,0},{9,1},... | collective-permute-start | bytes 786440 | tf_op jit(solution)/shard_map/ppermute | solution.py:681
  189.8 18.8 %collective-permute-start.26 = (f32[32,2048]{1,0:T(8,128)S(1)}, f32[32,2048]{1,0:T(8,128)S(1)}, u32[]{:S(2)}, u32[]{:S(2)}) collective-permute-start(f32[32,2048]{1,0:T(8,128)S(1)} %add.33.own_ref), channel_id=1, source_target_pairs={{0,8},{1,9},{2,10},{3,11},{4,12},{5,13},{6,14},{7,15},{8,0},{9,1},... | collective-permute-start | bytes 786440 | tf_op jit(solution)/shard_map/ppermute | solution.py:681
  190.6 18.1 %collective-permute-start.19 = (f32[160,128]{1,0:T(8,128)S(1)}, f32[160,128]{1,0:T(8,128)S(1)}, u32[]{:S(2)}, u32[]{:S(2)}) collective-permute-start(f32[160,128]{1,0:T(8,128)S(1)} %get-tuple-element.322), channel_id=1, source_target_pairs={{0,8},{1,9},{2,10},{3,11},{4,12},{5,13},{6,14},{7,15},{8,0},{9,1},... | collective-permute-start | bytes 245768 | tf_op jit(solution)/shard_map/ppermute | solution.py:681
  209.2 16.4 %collective-permute-start.29 = (f32[1024,512]{1,0:T(8,128)S(1)}, f32[1024,512]{1,0:T(8,128)S(1)}, u32[]{:S(2)}, u32[]{:S(2)}) collective-permute-start(f32[1024,512]{1,0:T(8,128)S(1)} %shard_map.319.own_ref), channel_id=1, source_target_pairs={{0,1},{1,0},{2,3},{3,2},{4,5},{5,4},{6,7},{7,6},{8,9},{9,8},{10,11... | collective-permute-start | bytes 6291464 | tf_op jit(solution)/shard_map/ppermute | solution.py:681
  209.2 18.4 %collective-permute-start.27 = (f32[64,2048]{1,0:T(8,128)S(1)}, f32[64,2048]{1,0:T(8,128)S(1)}, u32[]{:S(2)}, u32[]{:S(2)}) collective-permute-start(f32[64,2048]{1,0:T(8,128)S(1)} %shard_map.318.own_ref), channel_id=1, source_target_pairs={{0,4},{1,3},{2,6},{3,1},{4,0},{5,7},{6,2},{7,5},{8,12},{9,11},{10,... | collective-permute-start | bytes 1572872 | tf_op jit(solution)/shard_map/ppermute | solution.py:681
  209.7 15.9 %collective-permute-start.28 = (f32[128,512]{1,0:T(8,128)S(1)}, f32[128,512]{1,0:T(8,128)S(1)}, u32[]{:S(2)}, u32[]{:S(2)}) collective-permute-start(f32[128,512]{1,0:T(8,128)S(1)} %add.34), channel_id=1, source_target_pairs={{0,16},{1,17},{2,18},{3,19},{4,20},{5,21},{6,22},{7,23},{8,24},{9,... | collective-permute-start | bytes 786440 | tf_op jit(solution)/shard_map/ppermute | solution.py:681
  227.8 24.2 %collective-permute-start.34 = (f32[128,2048]{1,0:T(8,128)S(1)}, f32[128,2048]{1,0:T(8,128)S(1)}, u32[]{:S(2)}, u32[]{:S(2)}) collective-permute-start(f32[128,2048]{1,0:T(8,128)S(1)} %shard_map.321.own_ref), channel_id=1, source_target_pairs={{0,2},{1,5},{2,0},{3,7},{4,6},{5,1},{6,4},{7,3},{8,10},{9,13},{10,... | collective-permute-start | bytes 3145736 | tf_op jit(solution)/shard_map/ppermute | solution.py:681
  228.8 14.1 %collective-permute-start.24 = (f32[128,512]{1,0:T(8,128)S(1)}, f32[128,512]{1,0:T(8,128)S(1)}, u32[]{:S(2)}, u32[]{:S(2)}) collective-permute-start(f32[128,512]{1,0:T(8,128)S(1)} %add.35), channel_id=1, source_target_pairs={{0,16},{1,17},{2,18},{3,19},{4,20},{5,21},{6,22},{7,23},{8,24},{9,... | collective-permute-start | bytes 786440 | tf_op jit(solution)/shard_map/ppermute | solution.py:681
  228.8 15.9 %collective-permute-start.32 = (f32[128,512]{1,0:T(8,128)S(1)}, f32[128,512]{1,0:T(8,128)S(1)}, u32[]{:S(2)}, u32[]{:S(2)}) collective-permute-start(f32[128,512]{1,0:T(8,128)S(1)} %add.37.own_ref), channel_id=1, source_target_pairs={{0,8},{1,9},{2,10},{3,11},{4,12},{5,13},{6,14},{7,15},{8,0},{9,1},... | collective-permute-start | bytes 786440 | tf_op jit(solution)/shard_map/ppermute | solution.py:681
  252.2 12.5 %collective-permute-start.37 = (f32[256,2048]{1,0:T(8,128)S(1)}, f32[256,2048]{1,0:T(8,128)S(1)}, u32[]{:S(2)}, u32[]{:S(2)}) collective-permute-start(f32[256,2048]{1,0:T(8,128)S(1)} %shard_map.324.own_ref), channel_id=1, source_target_pairs={{0,1},{1,0},{2,3},{3,2},{4,5},{5,4},{6,7},{7,6},{8,9},{9,8},{10,11... | collective-permute-start | bytes 6291464 | tf_op jit(solution)/shard_map/ppermute | solution.py:681
  261.8 22.2 %collective-permute-start.40 = (f32[512,512]{1,0:T(8,128)S(1)}, f32[512,512]{1,0:T(8,128)S(1)}, u32[]{:S(2)}, u32[]{:S(2)}) collective-permute-start(f32[512,512]{1,0:T(8,128)S(1)} %shard_map.326.own_ref), channel_id=1, source_target_pairs={{0,2},{1,5},{2,0},{3,7},{4,6},{5,1},{6,4},{7,3},{8,10},{9,13},{10,... | collective-permute-start | bytes 3145736 | tf_op jit(solution)/shard_map/ppermute | solution.py:681
  262.6 14.9 %collective-permute-start.36 = (f32[256,512]{1,0:T(8,128)S(1)}, f32[256,512]{1,0:T(8,128)S(1)}, u32[]{:S(2)}, u32[]{:S(2)}) collective-permute-start(f32[256,512]{1,0:T(8,128)S(1)} %shard_map.323.own_ref), channel_id=1, source_target_pairs={{0,4},{1,3},{2,6},{3,1},{4,0},{5,7},{6,2},{7,5},{8,12},{9,11},{10,... | collective-permute-start | bytes 1572872 | tf_op jit(solution)/shard_map/ppermute | solution.py:681
  264.6 16.4 %collective-permute-start.35 = (f32[320,128]{1,0:T(8,128)S(1)}, f32[320,128]{1,0:T(8,128)S(1)}, u32[]{:S(2)}, u32[]{:S(2)}) collective-permute-start(f32[320,128]{1,0:T(8,128)S(1)} %shard_map.325.own_ref), channel_id=1, source_target_pairs={{0,4},{1,3},{2,6},{3,1},{4,0},{5,7},{6,2},{7,5},{8,12},{9,11},{10,... | collective-permute-start | bytes 491528 | tf_op jit(solution)/shard_map/ppermute | solution.py:681
  284.3 14.9 %collective-permute-start.39 = (f32[512,512]{1,0:T(8,128)S(1)}, f32[512,512]{1,0:T(8,128)S(1)}, u32[]{:S(2)}, u32[]{:S(2)}) collective-permute-start(f32[512,512]{1,0:T(8,128)S(1)} %shard_map.328.own_ref), channel_id=1, source_target_pairs={{0,2},{1,5},{2,0},{3,7},{4,6},{5,1},{6,4},{7,3},{8,10},{9,13},{10,... | collective-permute-start | bytes 3145736 | tf_op jit(solution)/shard_map/ppermute | solution.py:681
  (37 other events, 253.3 us)
where the time goes:
time: 317 us; the launch traced here: 316 us
  Pallas kernels  134 us (42%)
  waiting for transfers between devices  126 us (40%)
  starting transfers between devices  51.8 us (16%)
    ppermute x45, waiting for transfers between devices, swap(): return lax.ppermute(values, 'dp', moves)  126 us
    pallas_call x1, Pallas kernels, run_forward(): pl.pallas_call(functools.partial(forward_kernel, lax.axis_size('dp'), nta...  57.2 us
    ppermute x45, starting transfers between devices, swap(): return lax.ppermute(values, 'dp', moves)  51.8 us
    pallas_call x2, Pallas kernels, call_rows(): pl.pallas_call(kernel, grid=(rows,), in_specs=[spec(*item) for item in in...  44.7 us
    pallas_call x20, Pallas kernels, join_parts(): pl.pallas_call(functools.partial(join_kernel, bits, cuts), in_specs=[any_...  11.2 us
    pallas_call x15, Pallas kernels, add_parts(): pl.pallas_call(functools.partial(add_kernel, bits), out_shape=[half, half...  9.86 us
  transfers between devices with their start and end apart: 45, of which 24 were waited for; matrix products, arithmetic and copies ran while one was open for 0% of the time, Pallas kernels for 20%

commit v1 on v0

--- a/solution.py
+++ b/solution.py
@@ -194,13 +194,13 @@
     allowed = jnp.logical_and(keys <= queries, segment_q == segment)
     bias_ref[...] = jnp.where(allowed, 0.0, -1e9)
 
-    def attend_row(q_ref, k_ref, v_ref, masked, mixed_ref, share_ref, prob_ref):
+    def attend_row(q_ref, k_ref, v_ref, masked, mixed_ref, share_ref, prob_ref, before):
         copies = []
         for pair in range(PAIRS):
             lanes = slice(pair * LANES, (pair + 1) * LANES)
-            slot = pair % 2
-            if pair >= 2:
-                copies[pair - 2].wait()
+            slot = pair
+            if before:
+                before[pair].wait()
             pair_k = k_ref[0, :, lanes]
             pair_v = v_ref[0, :, lanes]
             ones = jnp.concatenate([pair_v, jnp.ones_like(pair_v)], axis=1)
@@ -220,10 +220,9 @@
             )
             copy.start()
             copies.append(copy)
-        copies[PAIRS - 2].wait()
-        copies[PAIRS - 1].wait()
-
-    attend_row(q_ref, k_ref, v_ref, True, mixed_one_ref, share_one_ref, prob_one_ref)
+        return copies
+
+    copies = attend_row(q_ref, k_ref, v_ref, True, mixed_one_ref, share_one_ref, prob_one_ref, [])
 
     branch = dot(mixed_one_ref[0], self_out_ref[...])
     branch_low = branch.astype(bf16)
@@ -237,7 +236,7 @@
     in_two_ref[0] = in_two
     cq_ref[0] = (dot(in_two, cross_qkv_ref[0]).astype(bf16).astype(f32) * 0.125).astype(bf16)
 
-    attend_row(cq_ref, ck_ref, cv_ref, False, mixed_two_ref, share_two_ref, prob_two_ref)
+    copies = attend_row(cq_ref, ck_ref, cv_ref, False, mixed_two_ref, share_two_ref, prob_two_ref, copies)
 
     after_two = after_one_ref[0] + dot(mixed_two_ref[0], cross_out_ref[...])
     after_two_ref[...] = after_two
@@ -286,6 +285,8 @@
         for copy in halves(ffn_out_grad_ref, out_kept_ref, out_sent_ref, part_sem, 0):
             copy.start()
 
+    for copy in copies:
+        copy.wait()
     in_three_t = in_three.T
     d_in = None
     for c in range(4):
@@ -352,8 +353,8 @@
         out_specs=[spec for spec, _ in outs],
         out_shape=[shape for _, shape in outs],
         scratch_shapes=[
-            pltpu.VMEM((64, LANES), f32), pltpu.VMEM((seq, seq), f32), pltpu.VMEM((2, 2, seq, seq), bf16),
-            pltpu.SemaphoreType.DMA((2,)), pltpu.VMEM((seq, ff), bf16), pltpu.VMEM((seq, ff), f32),
+            pltpu.VMEM((64, LANES), f32), pltpu.VMEM((seq, seq), f32), pltpu.VMEM((PAIRS, 2, seq, seq), bf16),
+            pltpu.SemaphoreType.DMA((PAIRS,)), pltpu.VMEM((seq, ff), bf16), pltpu.VMEM((seq, ff), f32),
             pltpu.VMEM((seq, width), f32),
             pltpu.VMEM((width, ff), f32), pltpu.VMEM((ff, width), f32), pltpu.SemaphoreType.DMA((4,)),
         ],
@@ -399,35 +400,55 @@
                 out_ref[256:, lanes] = both[:, 256:].T.astype(bf16)
 
 
+def heads_back_kernel(
+    masked, grad_ref, mixed_ref, q_ref, k_ref, v_ref, share_ref, prob_ref, out_ref,
+    dq_ref, dk_ref, dv_ref, out_grad_ref, d_mixed_ref,
+):
+    @pl.when(pl.program_id(0) == 0)
+    def _():
+        out_grad_ref[...] = jnp.zeros_like(out_grad_ref)
+
+    grad_low = grad_ref[0].astype(bf16)
+    out_grad_ref[...] += dot_tn(mixed_ref[0], grad_low)
+    d_mixed_ref[...] = dot_nt(grad_low, out_ref[...]).astype(bf16)
+    attend_back(
+        q_ref, k_ref, v_ref, mixed_ref, share_ref, prob_ref, d_mixed_ref, masked,
+        dq_ref.at[0], dk_ref.at[0], dv_ref.at[0],
+    )
+
+
 def cross_back_kernel(
-    grad_two_ref, mixed_ref, q_ref, k_ref, v_ref, share_ref, prob_ref, mem_ref, in_two_ref, after_one_ref,
-    narrow_ref, branch_ref, gains_ref, down_w_ref, up_w_ref, cross_qkv_ref, cross_out_ref,
+    grad_two_ref, dq_ref, dk_ref, dv_ref, out_grad_ref, mem_ref, in_two_ref, after_one_ref,
+    narrow_ref, branch_ref, gains_ref, down_w_ref, up_w_ref, cross_qkv_ref,
     kept_ref, sent_ref, mem_grad_ref, grad_one_ref, d_branch_ref, up_grad_ref, down_grad_ref, gain_grad_ref,
-    d_mixed_ref, dq_ref, dk_ref, dv_ref, total_ref, part_sem,
+    total_ref, part_sem,
 ):
     row = pl.program_id(0)
+    last = row == pl.num_programs(0) - 1
+    dq, dk, dv = dq_ref[0], dk_ref[0], dv_ref[0]
+    memory_t = mem_ref[0].T
+    terms = (dot_tn(in_two_ref[0], dq), dot(memory_t, dk), dot(memory_t, dv))
 
     @pl.when(row == 0)
     def _():
-        for ref in (total_ref, up_grad_ref, down_grad_ref, gain_grad_ref):
+        for ref in (up_grad_ref, down_grad_ref, gain_grad_ref):
             ref[...] = jnp.zeros_like(ref)
-
-    grad_low = grad_two_ref[0].astype(bf16)
-    total_ref[0:512] += dot_tn(mixed_ref[0], grad_low)
-    d_mixed_ref[...] = dot_nt(grad_low, cross_out_ref[...]).astype(bf16)
-    attend_back(q_ref, k_ref, v_ref, mixed_ref, share_ref, prob_ref, d_mixed_ref, False, dq_ref, dk_ref, dv_ref)
-    total_ref[512:1024] += dot_tn(in_two_ref[0], dq_ref[...])
-    memory_t = mem_ref[0].T
-    total_ref[1024:1536] += dot(memory_t, dk_ref[...])
-    total_ref[1536:2048] += dot(memory_t, dv_ref[...])
-
-    @pl.when(row == pl.num_programs(0) - 1)
+        total_ref[:512] = out_grad_ref[...]
+        for i, term in enumerate(terms):
+            total_ref[(1 + i) * 512 : (2 + i) * 512] = term
+
+    @pl.when(row > 0)
+    def _():
+        for i, term in enumerate(terms):
+            total_ref[(1 + i) * 512 : (2 + i) * 512] += term
+
+    @pl.when(last)
     def _():
         for copy in halves(total_ref, kept_ref, sent_ref, part_sem, 0):
             copy.start()
 
-    mem_grad_ref[0] = dot_nt(dk_ref[...], cross_qkv_ref[1]) + dot_nt(dv_ref[...], cross_qkv_ref[2])
-    d_in = dot_nt(dq_ref[...], cross_qkv_ref[0])
+    mem_grad_ref[0] = dot_nt(dk, cross_qkv_ref[1]) + dot_nt(dv, cross_qkv_ref[2])
+    d_in = dot_nt(dq, cross_qkv_ref[0])
     after_one = after_one_ref[0]
     d_after, gain_grad = rms_back(after_one, rms_inv(after_one), gains_ref[1, 0:1], d_in)
     gain_grad_ref[...] += jnp.broadcast_to(gain_grad, gain_grad_ref.shape)
@@ -442,47 +463,49 @@
     down_grad_ref[...] += dot_tn(d_narrow, branch_ref[0])[:RANK]
     d_branch_ref[0] = (grad + dot_nt(d_narrow, down_w_ref[0])).astype(bf16)
 
-    @pl.when(row == pl.num_programs(0) - 1)
+    @pl.when(last)
     def _():
         for copy in halves(total_ref, kept_ref, sent_ref, part_sem, 0):
             copy.wait()
 
 
 def self_back_kernel(
-    d_branch_ref, mixed_ref, q_ref, k_ref, v_ref, share_ref, prob_ref, in_one_ref, x_ref, grad_one_ref, gains_ref,
-    self_qkv_ref, self_out_ref,
+    dq_ref, dk_ref, dv_ref, out_grad_ref, in_one_ref, x_ref, grad_one_ref, gains_ref, self_qkv_ref,
     kept_ref, sent_ref, input_grad_ref, gain_grad_ref,
-    d_mixed_ref, dq_ref, dk_ref, dv_ref, total_ref, part_sem,
+    total_ref, part_sem,
 ):
     row = pl.program_id(0)
+    last = row == pl.num_programs(0) - 1
+    in_one_t = in_one_ref[0].T
+    terms = [dot(in_one_t, ref[0]) for ref in (dq_ref, dk_ref, dv_ref)]
 
     @pl.when(row == 0)
     def _():
-        for ref in (total_ref, gain_grad_ref):
-            ref[...] = jnp.zeros_like(ref)
-
-    total_ref[0:512] += dot_tn(mixed_ref[0], d_branch_ref[0])
-    d_mixed_ref[...] = dot_nt(d_branch_ref[0], self_out_ref[...]).astype(bf16)
-    attend_back(q_ref, k_ref, v_ref, mixed_ref, share_ref, prob_ref, d_mixed_ref, True, dq_ref, dk_ref, dv_ref)
-    in_one_t = in_one_ref[0].T
-    for j, ref in enumerate((dq_ref, dk_ref, dv_ref)):
-        total_ref[(1 + j) * 512 : (2 + j) * 512] += dot(in_one_t, ref[...])
-
-    @pl.when(row == pl.num_programs(0) - 1)
+        gain_grad_ref[...] = jnp.zeros_like(gain_grad_ref)
+        total_ref[:512] = out_grad_ref[...]
+        for i, term in enumerate(terms):
+            total_ref[(1 + i) * 512 : (2 + i) * 512] = term
+
+    @pl.when(row > 0)
+    def _():
+        for i, term in enumerate(terms):
+            total_ref[(1 + i) * 512 : (2 + i) * 512] += term
+
+    @pl.when(last)
     def _():
         for copy in halves(total_ref, kept_ref, sent_ref, part_sem, 0):
             copy.start()
 
     d_in = None
     for j, ref in enumerate((dq_ref, dk_ref, dv_ref)):
-        part = dot_nt(ref[...], self_qkv_ref[j])
+        part = dot_nt(ref[0], self_qkv_ref[j])
         d_in = part if d_in is None else d_in + part
     x = x_ref[0].astype(f32)
     d_x, gain_grad = rms_back(x, rms_inv(x), gains_ref[0, 0:1], d_in)
     gain_grad_ref[...] += jnp.broadcast_to(gain_grad, gain_grad_ref.shape)
     input_grad_ref[0] = grad_one_ref[0] + d_x
 
-    @pl.when(row == pl.num_programs(0) - 1)
+    @pl.when(last)
     def _():
         for copy in halves(total_ref, kept_ref, sent_ref, part_sem, 0):
             copy.wait()
@@ -657,8 +680,13 @@
     )(own, got)
 
 
-SEQUENCE = "01A012B0213C03442013014203410234102013243142134223434D"
-ORDER = ((1, 1), (2, 4), (4, 2), (8, 8), (16, 16))
+SEQUENCE = "A1001a0B1022b103C32014102423401323241340042433121243344D"
+ORDERS = {
+    "P": ((1, 1), (2, 4), (4, 2), (8, 8), (16, 16)),
+    "Q": ((1, 1), (4, 2), (2, 4), (8, 8), (16, 16)),
+    "R": ((1, 1), (4, 2), (8, 8), (16, 16), (2, 4)),
+    "S": ((1, 1), (2, 4), (8, 8), (16, 16), (4, 2)),
+}
 
 
 class Line:
@@ -672,7 +700,7 @@
         return values
 
 
-def summing(kept, sent, cuts, line, found):
+def summing(kept, sent, cuts, line, found, order):
     devices = lax.axis_size("dp")
     state = {}
 
@@ -686,16 +714,16 @@
 
     high = [(32 << i, 32 << i) for i in range(max(devices // 32, 1).bit_length() - 1)]
     sent = line.tie(sent)
-    got = swap(sent, ORDER[0])
+    got = swap(sent, order[0])
     mark(kept)
     yield
-    for bits in ORDER[1:-1]:
+    for bits in order[1:-1]:
         got = line.tie(got)
         sent, kept = add_parts(state["kept"], got, bits)
         got = swap(sent, bits)
         mark(kept)
         yield
-    for bits in list(ORDER[-1:]) + high:
+    for bits in list(order[-1:]) + high:
         got = line.tie(got)
         total = state["kept"] + got
         got = swap(total, bits)
@@ -703,16 +731,16 @@
         yield
     got = line.tie(got)
     total = state["kept"] + got
-    for bits in ORDER[:-1][::-1]:
+    for bits in order[:-1][::-1]:
         got = swap(total, bits)
         mark(total)
         yield
         got = line.tie(got)
         own = state["kept"]
-        if bits == ORDER[0]:
+        if bits == order[0]:
             break
         (total,) = join_parts(own, got, bits, (2 * own.shape[0],))
-    parts = join_parts(own, got, ORDER[0], cuts)
+    parts = join_parts(own, got, order[0], cuts)
     mark(parts[-1])
     found.append((parts[:-1], state))
 
@@ -736,15 +764,15 @@
     ) = run_forward(tokens, memory, segments, cotangent, group_sizes, params)
     like = lambda shape, dtype=f32: jax.ShapeDtypeStruct(shape, dtype)
     wide = tokens.shape
-    row_scratch = [pltpu.VMEM((seq, width), bf16)] * 4
-    row_scratch += [pltpu.VMEM((4 * width, width), f32), pltpu.SemaphoreType.DMA((2,))]
+    row_scratch = [pltpu.VMEM((seq, width), bf16)]
+    total_scratch = [pltpu.VMEM((4 * width, width), f32), pltpu.SemaphoreType.DMA((2,))]
     pair = (2 * width, width)
     line = Line()
     sums = [[] for _ in range(5)]
     ff = ffn_out.shape[0]
 
     def start(which, kept, sent, cuts):
-        return summing(kept, sent, cuts, line, sums[which])
+        return summing(kept, sent, cuts, line, sums[which], ORDERS["QQQQP"[which]])
 
     def mark(value):
         line.last = {"kept": value}
@@ -756,34 +784,59 @@
             next(chunks[step], None)
         elif step == "A":
             grad_two = line.tie(grad_two)
+            dq, dk, dv, out_grad = call_rows(
+                functools.partial(heads_back_kernel, False),
+                rows,
+                [
+                    (grad_two, True), (mixed_two, True), (q_two, True), (k_two, True), (v_two, True),
+                    (share_two, True), (prob_two, True), (cross_out, False),
+                ],
+                [(like(wide, bf16), True)] * 3 + [(like(cross_out.shape), False)],
+                row_scratch,
+            )
+            held = mark(dq)
+        elif step == "a":
+            dq = line.tie(held["kept"])
             cross_kept, cross_sent, memory_grad, grad_one, d_branch, up_one, down_one, gain_two = call_rows(
                 cross_back_kernel,
                 rows,
                 [
-                    (grad_two, True), (mixed_two, True), (q_two, True), (k_two, True), (v_two, True), (share_two, True),
-                    (prob_two, True), (memory, True), (in_two, True), (after_one, True), (narrow, True), (branch, True),
-                    (gains, False), (down_w, False), (up_w, False), (cross_qkv, False), (cross_out, False),
+                    (grad_two, True), (dq, True), (dk, True), (dv, True), (out_grad, False), (memory, True),
+                    (in_two, True), (after_one, True), (narrow, True), (branch, True),
+                    (gains, False), (down_w, False), (up_w, False), (cross_qkv, False),
                 ],
                 [
-                    (like(pair), None), (like(pair), None), (like(wide), True), (like(wide), True),
-                    (like(wide, bf16), True), (like((RANK, width)), False), (like((RANK, width)), False), (like((8, width)), False),
+                    (like(pair), None), (like(pair), None), (like(wide), True), (like(wide), True), (like(wide, bf16), True),
+                    (like((RANK, width)), False), (like((RANK, width)), False), (like((8, width)), False),
                 ],
-                row_scratch,
+                total_scratch,
             )
             memory_grad = mark(memory_grad)
             chunks["2"] = start(2, cross_kept, cross_sent, (width, 3 * width))
         elif step == "B":
             d_branch = line.tie(d_branch)
+            dq, dk, dv, out_grad = call_rows(
+                functools.partial(heads_back_kernel, True),
+                rows,
+                [
+                    (d_branch, True), (mixed_one, True), (q_one, True), (k_one, True), (v_one, True),
+                    (share_one, True), (prob_one, True), (self_out, False),
+                ],
+                [(like(wide, bf16), True)] * 3 + [(like(self_out.shape), False)],
+                row_scratch,
+            )
+            held = mark(dq)
+        elif step == "b":
+            dq = line.tie(held["kept"])
             self_kept, self_sent, input_grad, gain_one = call_rows(
                 self_back_kernel,
                 rows,
                 [
-                    (d_branch, True), (mixed_one, True), (q_one, True), (k_one, True), (v_one, True), (share_one, True),
-                    (prob_one, True), (in_one, True), (tokens, True), (grad_one, True), (gains, False),
-                    (self_qkv, False), (self_out, False),
+                    (dq, True), (dk, True), (dv, True), (out_grad, False), (in_one, True), (tokens, True),
+                    (grad_one, True), (gains, False), (self_qkv, False),
                 ],
                 [(like(pair), None), (like(pair), None), (like(wide), True), (like((8, width)), False)],
-                row_scratch,
+                total_scratch,
             )
             input_grad = mark(input_grad)
             chunks["3"] = start(3, self_kept, self_sent, (width, 3 * width))

time: 317 us -> 286 us (0.902)
  waiting for transfers between devices: 126 us -> 90.2 us
  Pallas kernels: 134 us -> 139 us
    ppermute x45, waiting for transfers between devices: 126 us -> 90.2 us  [swap(): return lax.ppermute(values, 'dp', moves)]
    pallas_call x2 -> x4, Pallas kernels: 44.7 us -> 55.2 us  [call_rows(): pl.pallas_call(kernel, grid=(rows,), in_specs=[spec(*item) for item in in...]
    pallas_call x1, Pallas kernels: 57.2 us -> 52.6 us  [run_forward(): pl.pallas_call(functools.partial(forward_kernel, lax.axis_size('dp'), nta...]
  transfers between devices with their start and end apart: 45 -> 45, of which waited for: 24 -> 24; matrix products, arithmetic and copies ran while one was open for 0% -> 0% of each run, Pallas kernels for 20% -> 28%
where the time goes in v1:
time: 286 us
  Pallas kernels  139 us (49%)
  waiting for transfers between devices  90.2 us (32%)
  starting transfers between devices  50.5 us (18%)
    ppermute x45, waiting for transfers between devices, swap(): return lax.ppermute(values, 'dp', moves)  90.2 us
    pallas_call x4, Pallas kernels, call_rows(): pl.pallas_call(kernel, grid=(rows,), in_specs=[spec(*item) for item in in...  55.2 us
    pallas_call x1, Pallas kernels, run_forward(): pl.pallas_call(functools.partial(forward_kernel, lax.axis_size('dp'), nta...  52.6 us
    ppermute x45, starting transfers between devices, swap(): return lax.ppermute(values, 'dp', moves)  50.5 us
    pallas_call x20, Pallas kernels, join_parts(): pl.pallas_call(functools.partial(join_kernel, bits, cuts), in_specs=[any_...  11.2 us
    pallas_call x15, Pallas kernels, add_parts(): pl.pallas_call(functools.partial(add_kernel, bits), out_shape=[half, half...  9.4 us
    pallas_call x1, Pallas kernels, on_device(): pl.pallas_call(functools.partial(spread_kernel, ntask), out_shape=[like(i...  5.83 us
  transfers between devices with their start and end apart: 45, of which 24 were waited for; matrix products, arithmetic and copies ran while one was open for 0% of the time, Pallas kernels for 28%

profile of v1, /device:TPU:0, one launch (start us, length us, event | category | flops | bytes accessed | tf_op | source)
XLA Modules:
  0.0 285.6 jit_solution(7992324977221320644)
XLA Ops:
  0.6 52.6 %shard_map.297 = (bf16[2,512,512]{2,1,0:T(8,128)(2,1)}, f32[2,512,512]{2,1,0:T(8,128)}, f32[256,2048]{1,0:T(8,128)}, f32[256,2048]{1,0:T(8,128)}, f32[1024,512]{...) custom-call(s32[8]{0:T(128)} %sizes_ref.3, ...), custom_call_target="tpu_custom_call" | custom-call | flops 1 | bytes 1 | tf_op jit(solution)/shard_map/pallas_call | solution.py:346
  53.8 16.6 %shard_map.298 = (bf16[2,512,512]{2,1,0:T(8,128)(2,1)}, bf16[2,512,512]{2,1,0:T(8,128)(2,1)}, bf16[2,512,512]{2,1,0:T(8,128)(2,1)}, f32[512,512]{1,0:T(8,128)}) custom-call(f32[2,512,512]{2,1,0:T(8,128)} %get-tuple-element.219.grad_ref.grad_two_ref, bf16[2,512,512]{2,1,0:T(8,128)(2,1)} %get-tuple-element.220.mixed_ref, ...), custom_call_target="tpu_custom_call" | custom-call | flops 1 | bytes 1 | tf_op jit(solution)/shard_map/pallas_call | solution.py:613
  70.4 3.0 %shard_map.299 = (f32[512,512]{1,0:T(8,128)}, f32[512,512]{1,0:T(8,128)S(1)}) custom-call(f32[1024,512]{1,0:T(8,128)S(1)} %copy-done.5, f32[1024,512]{1,0:T(8,128)} %collective-permute-done.1.got_ref), custom_call_target="tpu_custom_call" | custom-call | flops 1 | bytes 1 | tf_op jit(solution)/shard_map/pallas_call | solution.py:662
  73.5 3.0 %collective-permute-start.3 = (f32[512,512]{1,0:T(8,128)}, f32[512,512]{1,0:T(8,128)}, u32[]{:S(2)}, u32[]{:S(2)}) collective-permute-start(f32[512,512]{1,0:T(8,128)} %get-tuple-element.254), channel_id=1, source_target_pairs={{0,4},{1,3},{2,6},{3,1},{4,0},{5,7},{6,2},{7,5},{8,12},{9,11},{10,... | collective-permute-start | bytes 3145736 | tf_op jit(solution)/shard_map/ppermute | solution.py:709
  78.6 14.3 %shard_map.301 = (f32[1024,512]{1,0:T(8,128)}, f32[1024,512]{1,0:T(8,128)}, f32[2,512,512]{2,1,0:T(8,128)}, f32[2,512,512]{2,1,0:T(8,128)}, bf16[2,512,512]{2,1,...) custom-call(f32[2,512,512]{2,1,0:T(8,128)} %get-tuple-element.219.grad_ref.grad_two_ref, ...), custom_call_target="tpu_custom_call" | custom-call | flops 1 | bytes 1 | tf_op jit(solution)/shard_map/pallas_call | solution.py:613
  92.9 2.1 shard_map.302
  96.6 13.3 %shard_map.303 = (bf16[2,512,512]{2,1,0:T(8,128)(2,1)}, bf16[2,512,512]{2,1,0:T(8,128)(2,1)}, bf16[2,512,512]{2,1,0:T(8,128)(2,1)}, f32[512,512]{1,0:T(8,128)}) custom-call(bf16[2,512,512]{2,1,0:T(8,128)(2,1)} %get-tuple-element.258.grad_ref, bf16[2,512,512]{2,1,0:T(8,128)(2,1)} %get-tuple-element.259.mixed_ref, ...), custom_call_target="tpu_custom_call" | custom-call | flops 1 | bytes 1 | tf_op jit(solution)/shard_map/pallas_call | solution.py:613
  114.2 2.2 collective-permute-done.6.got_ref
  117.7 11.0 %shard_map.307 = (f32[1024,512]{1,0:T(8,128)}, f32[1024,512]{1,0:T(8,128)}, f32[2,512,512]{2,1,0:T(8,128)}, f32[8,512]{1,0:T(8,128)}) custom-call(bf16[2,512,512]{2,1,0:T(8,128)(2,1)} %get-tuple-element.280.dq_ref, bf16[2,512,512]{2,1,0:T(8,128)(2,1)} %get-tuple-element.281.dk_ref, bf16[2,512,512]{2,1,0:T(8,128)(2,1)} %get-tuple-element.282.dv_ref, ...), custom_call_target="tpu_custom_call" | custom-call | flops 1 | bytes 1 | tf_op jit(solution)/shard_map/pallas_call | solution.py:613
  131.2 2.6 collective-permute-start.9
  136.2 5.0 %shard_map.309 = (f32[1280,128]{1,0:T(8,128)S(1)}, f32[1280,128]{1,0:T(8,128)S(1)}) custom-call(s32[8]{0:T(128)S(1)} %copy-done.19, f32[16,512]{1,0:T(8,128)S(1)} %copy-done.11, f32[16,512]{1,0:T(8,128)S(1)} %copy-done.9, f32[16,512]{1,0:T(8,128)S(1)} %copy-done.12, f32[16,512]{1,0:T(8,128)S(1)} %copy-done.10, f32[8,512]{1,0:T(8,128)S(1)} %copy-done.15, ...), custom_call_target="tpu_custom_call" | custom-call | flops 1 | bytes 1 | tf_op jit(solution)/shard_map/pallas_call | solution.py:845
  142.6 2.6 collective-permute-done.10.got_ref
  148.8 2.5 collective-permute-start.12
  151.3 10.6 %collective-permute-done.13 = f32[32,2048]{1,0:T(8,128)S(1)} collective-permute-done((f32[32,2048]{1,0:T(8,128)S(1)}, f32[32,2048]{1,0:T(8,128)S(1)}, u32[]{:S(2)}, u32[]{:S(2)}) %collective-permute-start.13) | collective-permute-done | bytes 262176 | tf_op jit(solution)/shard_map/ppermute | solution.py:709
  165.6 5.6 %collective-permute-done.16 = f32[128,512]{1,0:T(8,128)S(1)} collective-permute-done((f32[128,512]{1,0:T(8,128)S(1)}, f32[128,512]{1,0:T(8,128)S(1)}, u32[]{:S(2)}, u32[]{:S(2)}) %collective-permute-start.16) | collective-permute-done | bytes 262176 | tf_op jit(solution)/shard_map/ppermute | solution.py:709
  171.4 2.2 collective-permute-start.21
  177.3 2.4 collective-permute-start.24
  179.7 9.3 %collective-permute-done.22.got_ref = f32[32,2048]{1,0:T(8,128)S(1)} collective-permute-done((f32[32,2048]{1,0:T(8,128)S(1)}, f32[32,2048]{1,0:T(8,128)S(1)}, u32[]{:S(2)}, u32[]{:S(2)}) %collective-permute-start.22) | collective-permute-done | bytes 262176 | tf_op jit(solution)/shard_map/ppermute | solution.py:709
  191.9 7.1 %collective-permute-done.23 = f32[128,512]{1,0:T(8,128)S(1)} collective-permute-done((f32[128,512]{1,0:T(8,128)S(1)}, f32[128,512]{1,0:T(8,128)S(1)}, u32[]{:S(2)}, u32[]{:S(2)}) %collective-permute-start.23) | collective-permute-done | bytes 262176 | tf_op jit(solution)/shard_map/ppermute | solution.py:709
  199.0 3.4 %collective-permute-start.27 = (f32[128,512]{1,0:T(8,128)S(1)}, f32[128,512]{1,0:T(8,128)S(1)}, u32[]{:S(2)}, u32[]{:S(2)}) collective-permute-start(f32[128,512]{1,0:T(8,128)S(1)} %add.36), channel_id=1, source_target_pairs={{0,16},{1,17},{2,18},{3,19},{4,20},{5,21},{6,22},{7,23},{8,24},{9,... | collective-permute-start | bytes 786440 | tf_op jit(solution)/shard_map/ppermute | solution.py:709
  203.3 4.1 %collective-permute-done.25.got_ref = f32[128,512]{1,0:T(8,128)S(1)} collective-permute-done((f32[128,512]{1,0:T(8,128)S(1)}, f32[128,512]{1,0:T(8,128)S(1)}, u32[]{:S(2)}, u32[]{:S(2)}) %collective-permute-start.25) | collective-permute-done | bytes 262176 | tf_op jit(solution)/shard_map/ppermute | solution.py:709
  207.7 2.5 collective-permute-start.26
  210.4 2.3 collective-permute-done.26
  221.2 6.5 %collective-permute-done.30.got_ref = f32[256,512]{1,0:T(8,128)S(1)} collective-permute-done((f32[256,512]{1,0:T(8,128)S(1)}, f32[256,512]{1,0:T(8,128)S(1)}, u32[]{:S(2)}, u32[]{:S(2)}) %collective-permute-start.30) | collective-permute-done | bytes 524320 | tf_op jit(solution)/shard_map/ppermute | solution.py:709
  230.7 6.4 %collective-permute-done.34.got_ref = f32[160,128]{1,0:T(8,128)S(1)} collective-permute-done((f32[160,128]{1,0:T(8,128)S(1)}, f32[160,128]{1,0:T(8,128)S(1)}, u32[]{:S(2)}, u32[]{:S(2)}) %collective-permute-start.34) | collective-permute-done | bytes 81952 | tf_op jit(solution)/shard_map/ppermute | solution.py:709
  239.2 11.1 %collective-permute-done.35.got_ref = f32[256,512]{1,0:T(8,128)S(1)} collective-permute-done((f32[256,512]{1,0:T(8,128)S(1)}, f32[256,512]{1,0:T(8,128)S(1)}, u32[]{:S(2)}, u32[]{:S(2)}) %collective-permute-start.35) | collective-permute-done | bytes 524320 | tf_op jit(solution)/shard_map/ppermute | solution.py:709
  257.9 2.0 shard_map.332
  259.9 8.1 %collective-permute-done.37.got_ref = f32[320,128]{1,0:T(8,128)S(1)} collective-permute-done((f32[320,128]{1,0:T(8,128)S(1)}, f32[320,128]{1,0:T(8,128)S(1)}, u32[]{:S(2)}, u32[]{:S(2)}) %collective-permute-start.37) | collective-permute-done | bytes 163872 | tf_op jit(solution)/shard_map/ppermute | solution.py:709
  269.4 3.5 %collective-permute-done.43.got_ref = f32[1024,512]{1,0:T(8,128)S(1)} collective-permute-done((f32[1024,512]{1,0:T(8,128)S(1)}, f32[1024,512]{1,0:T(8,128)S(1)}, u32[]{:S(2)}, u32[]{:S(2)}) %collective-permute-start.43) | collective-permute-done | bytes 2097184 | tf_op jit(solution)/shard_map/ppermute | solution.py:709
  272.9 2.0 shard_map.335
  276.2 2.1 collective-permute-done.44.got_ref
  278.8 5.8 %shard_map.338 = (f32[8,64]{1,0:T(8,128)}, f32[2,64]{1,0:T(2,128)}, f32[64,128]{1,0:T(8,128)}, f32[128,64]{1,0:T(8,128)S(1)}, f32[64,1536]{1,0:T(8,128)}, /*index=5*/f32[64,8192]{1,0:T(8,128)}, f32[64,8192]{1,0:T(8,128)}) custom-call(f32[2560,128]{1,0:T(8,128)S(1)} %shard_map.337.sum_ref, f32[8,64]{1,0:T(8,128)S(1)} %copy-done.17, bf16[2,64]{1,0:T(2,128)(2,1)S(1)} %copy-done.20), custom_call_target="tpu_custom_call" | custom-call | flops 1 | bytes 1 | tf_op jit(solution)/shard_map/pallas_call | solution.py:866
  (155 shorter events, 55.9 us)
Async XLA Ops:
  53.3 17.2 %collective-permute-start.1 = (f32[1024,512]{1,0:T(8,128)}, f32[1024,512]{1,0:T(8,128)}, u32[]{:S(2)}, u32[]{:S(2)}) collective-permute-start(f32[1024,512]{1,0:T(8,128)} %get-tuple-element.232), channel_id=1, source_target_pairs={{0,1},{1,0},{2,3},{3,2},{4,5},{5,4},{6,7},{7,6},{8,9},{9,8},{10,11... | collective-permute-start | bytes 6291464 | tf_op jit(solution)/shard_map/ppermute | solution.py:709
  73.5 19.5 %collective-permute-start.3 = (f32[512,512]{1,0:T(8,128)}, f32[512,512]{1,0:T(8,128)}, u32[]{:S(2)}, u32[]{:S(2)}) collective-permute-start(f32[512,512]{1,0:T(8,128)} %get-tuple-element.254), channel_id=1, source_target_pairs={{0,4},{1,3},{2,6},{3,1},{4,0},{5,7},{6,2},{7,5},{8,12},{9,11},{10,... | collective-permute-start | bytes 3145736 | tf_op jit(solution)/shard_map/ppermute | solution.py:709
  77.6 32.3 %collective-permute-start.2 = (f32[128,2048]{1,0:T(8,128)}, f32[128,2048]{1,0:T(8,128)S(1)}, u32[]{:S(2)}, u32[]{:S(2)}) collective-permute-start(f32[128,2048]{1,0:T(8,128)} %get-tuple-element.240), channel_id=1, source_target_pairs={{0,4},{1,3},{2,6},{3,1},{4,0},{5,7},{6,2},{7,5},{8,12},{9,11},{10,... | collective-permute-start | bytes 3145736 | tf_op jit(solution)/shard_map/ppermute | solution.py:709
  95.1 15.8 %collective-permute-start.5 = (f32[256,512]{1,0:T(8,128)}, f32[256,512]{1,0:T(8,128)}, u32[]{:S(2)}, u32[]{:S(2)}) collective-permute-start(f32[256,512]{1,0:T(8,128)} %get-tuple-element.271), channel_id=1, source_target_pairs={{0,2},{1,5},{2,0},{3,7},{4,6},{5,1},{6,4},{7,3},{8,10},{9,13},{10,... | collective-permute-start | bytes 1572872 | tf_op jit(solution)/shard_map/ppermute | solution.py:709
  112.0 16.7 %collective-permute-start.4 = (f32[64,2048]{1,0:T(8,128)}, f32[64,2048]{1,0:T(8,128)S(1)}, u32[]{:S(2)}, u32[]{:S(2)}) collective-permute-start(f32[64,2048]{1,0:T(8,128)} %get-tuple-element.267), channel_id=1, source_target_pairs={{0,2},{1,5},{2,0},{3,7},{4,6},{5,1},{6,4},{7,3},{8,10},{9,13},{10,... | collective-permute-start | bytes 1572872 | tf_op jit(solution)/shard_map/ppermute | solution.py:709
  112.6 16.2 %collective-permute-start.8 = (f32[128,512]{1,0:T(8,128)S(1)}, f32[128,512]{1,0:T(8,128)}, u32[]{:S(2)}, u32[]{:S(2)}) collective-permute-start(f32[128,512]{1,0:T(8,128)S(1)} %get-tuple-element.294), channel_id=1, source_target_pairs={{0,8},{1,9},{2,10},{3,11},{4,12},{5,13},{6,14},{7,15},{8,0},{9,1},... | collective-permute-start | bytes 786440 | tf_op jit(solution)/shard_map/ppermute | solution.py:709
  130.0 11.3 %collective-permute-start.11 = (f32[1024,512]{1,0:T(8,128)}, f32[1024,512]{1,0:T(8,128)S(1)}, u32[]{:S(2)}, u32[]{:S(2)}) collective-permute-start(f32[1024,512]{1,0:T(8,128)} %get-tuple-element.303), channel_id=1, source_target_pairs={{0,1},{1,0},{2,3},{3,2},{4,5},{5,4},{6,7},{7,6},{8,9},{9,8},{10,11... | collective-permute-start | bytes 6291464 | tf_op jit(solution)/shard_map/ppermute | solution.py:709
  130.2 15.0 %collective-permute-start.10 = (f32[512,512]{1,0:T(8,128)}, f32[512,512]{1,0:T(8,128)S(1)}, u32[]{:S(2)}, u32[]{:S(2)}) collective-permute-start(f32[512,512]{1,0:T(8,128)} %copy-done.21), channel_id=1, source_target_pairs={{0,4},{1,3},{2,6},{3,1},{4,0},{5,7},{6,2},{7,5},{8,12},{9,11},{10,... | collective-permute-start | bytes 3145736 | tf_op jit(solution)/shard_map/ppermute | solution.py:709
  131.2 14.4 %collective-permute-start.9 = (f32[128,512]{1,0:T(8,128)S(1)}, f32[128,512]{1,0:T(8,128)S(1)}, u32[]{:S(2)}, u32[]{:S(2)}) collective-permute-start(f32[128,512]{1,0:T(8,128)S(1)} %add.30), channel_id=1, source_target_pairs={{0,16},{1,17},{2,18},{3,19},{4,20},{5,21},{6,22},{7,23},{8,24},{9,... | collective-permute-start | bytes 786440 | tf_op jit(solution)/shard_map/ppermute | solution.py:709
  133.8 12.0 %collective-permute-start.7 = (f32[32,2048]{1,0:T(8,128)S(1)}, f32[32,2048]{1,0:T(8,128)S(1)}, u32[]{:S(2)}, u32[]{:S(2)}) collective-permute-start(f32[32,2048]{1,0:T(8,128)S(1)} %get-tuple-element.291), channel_id=1, source_target_pairs={{0,8},{1,9},{2,10},{3,11},{4,12},{5,13},{6,14},{7,15},{8,0},{9,1},... | collective-permute-start | bytes 786440 | tf_op jit(solution)/shard_map/ppermute | solution.py:709
  141.5 29.8 %collective-permute-start.19 = (f32[512,512]{1,0:T(8,128)S(1)}, f32[512,512]{1,0:T(8,128)S(1)}, u32[]{:S(2)}, u32[]{:S(2)}) collective-permute-start(f32[512,512]{1,0:T(8,128)S(1)} %get-tuple-element.337), channel_id=1, source_target_pairs={{0,4},{1,3},{2,6},{3,1},{4,0},{5,7},{6,2},{7,5},{8,12},{9,11},{10,... | collective-permute-start | bytes 3145736 | tf_op jit(solution)/shard_map/ppermute | solution.py:709
  145.8 17.9 %collective-permute-start.17 = (f32[1280,128]{1,0:T(8,128)S(1)}, f32[1280,128]{1,0:T(8,128)S(1)}, u32[]{:S(2)}, u32[]{:S(2)}) collective-permute-start(f32[1280,128]{1,0:T(8,128)S(1)} %get-tuple-element.330), channel_id=1, source_target_pairs={{0,1},{1,0},{2,3},{3,2},{4,5},{5,4},{6,7},{7,6},{8,9},{9,8},{10,11... | collective-permute-start | bytes 1966088 | tf_op jit(solution)/shard_map/ppermute | solution.py:709
  145.9 17.7 %collective-permute-start.15 = (f32[256,512]{1,0:T(8,128)S(1)}, f32[256,512]{1,0:T(8,128)S(1)}, u32[]{:S(2)}, u32[]{:S(2)}) collective-permute-start(f32[256,512]{1,0:T(8,128)S(1)} %get-tuple-element.326), channel_id=1, source_target_pairs={{0,2},{1,5},{2,0},{3,7},{4,6},{5,1},{6,4},{7,3},{8,10},{9,13},{10,... | collective-permute-start | bytes 1572872 | tf_op jit(solution)/shard_map/ppermute | solution.py:709
  147.5 14.4 %collective-permute-start.13 = (f32[32,2048]{1,0:T(8,128)S(1)}, f32[32,2048]{1,0:T(8,128)S(1)}, u32[]{:S(2)}, u32[]{:S(2)}) collective-permute-start(f32[32,2048]{1,0:T(8,128)S(1)} %add.32), channel_id=1, source_target_pairs={{0,16},{1,17},{2,18},{3,19},{4,20},{5,21},{6,22},{7,23},{8,24},{9,... | collective-permute-start | bytes 786440 | tf_op jit(solution)/shard_map/ppermute | solution.py:709
  148.8 13.1 %collective-permute-start.12 = (f32[128,512]{1,0:T(8,128)S(1)}, f32[128,512]{1,0:T(8,128)S(1)}, u32[]{:S(2)}, u32[]{:S(2)}) collective-permute-start(f32[128,512]{1,0:T(8,128)S(1)} %add.31.own_ref), channel_id=1, source_target_pairs={{0,8},{1,9},{2,10},{3,11},{4,12},{5,13},{6,14},{7,15},{8,0},{9,1},... | collective-permute-start | bytes 786440 | tf_op jit(solution)/shard_map/ppermute | solution.py:709
  162.1 12.8 %collective-permute-start.14 = (f32[256,512]{1,0:T(8,128)S(1)}, f32[256,512]{1,0:T(8,128)S(1)}, u32[]{:S(2)}, u32[]{:S(2)}) collective-permute-start(f32[256,512]{1,0:T(8,128)S(1)} %shard_map.312.own_ref), channel_id=1, source_target_pairs={{0,2},{1,5},{2,0},{3,7},{4,6},{5,1},{6,4},{7,3},{8,10},{9,13},{10,... | collective-permute-start | bytes 1572872 | tf_op jit(solution)/shard_map/ppermute | solution.py:709
  163.8 11.0 %collective-permute-start.18 = (f32[640,128]{1,0:T(8,128)S(1)}, f32[640,128]{1,0:T(8,128)S(1)}, u32[]{:S(2)}, u32[]{:S(2)}) collective-permute-start(f32[640,128]{1,0:T(8,128)S(1)} %get-tuple-element.335), channel_id=1, source_target_pairs={{0,2},{1,5},{2,0},{3,7},{4,6},{5,1},{6,4},{7,3},{8,10},{9,13},{10,... | collective-permute-start | bytes 983048 | tf_op jit(solution)/shard_map/ppermute | solution.py:709
  171.4 18.2 %collective-permute-start.21 = (f32[256,512]{1,0:T(8,128)S(1)}, f32[256,512]{1,0:T(8,128)S(1)}, u32[]{:S(2)}, u32[]{:S(2)}) collective-permute-start(f32[256,512]{1,0:T(8,128)S(1)} %get-tuple-element.347), channel_id=1, source_target_pairs={{0,2},{1,5},{2,0},{3,7},{4,6},{5,1},{6,4},{7,3},{8,10},{9,13},{10,... | collective-permute-start | bytes 1572872 | tf_op jit(solution)/shard_map/ppermute | solution.py:709
  175.0 37.7 %collective-permute-start.31 = (f32[512,512]{1,0:T(8,128)S(1)}, f32[512,512]{1,0:T(8,128)S(1)}, u32[]{:S(2)}, u32[]{:S(2)}) collective-permute-start(f32[512,512]{1,0:T(8,128)S(1)} %shard_map.317.own_ref), channel_id=1, source_target_pairs={{0,4},{1,3},{2,6},{3,1},{4,0},{5,7},{6,2},{7,5},{8,12},{9,11},{10,... | collective-permute-start | bytes 3145736 | tf_op jit(solution)/shard_map/ppermute | solution.py:709
  176.0 12.9 %collective-permute-start.22 = (f32[32,2048]{1,0:T(8,128)S(1)}, f32[32,2048]{1,0:T(8,128)S(1)}, u32[]{:S(2)}, u32[]{:S(2)}) collective-permute-start(f32[32,2048]{1,0:T(8,128)S(1)} %add.33.own_ref), channel_id=1, source_target_pairs={{0,8},{1,9},{2,10},{3,11},{4,12},{5,13},{6,14},{7,15},{8,0},{9,1},... | collective-permute-start | bytes 786440 | tf_op jit(solution)/shard_map/ppermute | solution.py:709
  177.3 13.0 %collective-permute-start.24 = (f32[128,512]{1,0:T(8,128)S(1)}, f32[128,512]{1,0:T(8,128)S(1)}, u32[]{:S(2)}, u32[]{:S(2)}) collective-permute-start(f32[128,512]{1,0:T(8,128)S(1)} %add.34), channel_id=1, source_target_pairs={{0,16},{1,17},{2,18},{3,19},{4,20},{5,21},{6,22},{7,23},{8,24},{9,... | collective-permute-start | bytes 786440 | tf_op jit(solution)/shard_map/ppermute | solution.py:709
  189.2 21.0 %collective-permute-start.28 = (f32[64,2048]{1,0:T(8,128)S(1)}, f32[64,2048]{1,0:T(8,128)S(1)}, u32[]{:S(2)}, u32[]{:S(2)}) collective-permute-start(f32[64,2048]{1,0:T(8,128)S(1)} %shard_map.318.own_ref), channel_id=1, source_target_pairs={{0,2},{1,5},{2,0},{3,7},{4,6},{5,1},{6,4},{7,3},{8,10},{9,13},{10,... | collective-permute-start | bytes 1572872 | tf_op jit(solution)/shard_map/ppermute | solution.py:709
  189.7 9.3 %collective-permute-start.23 = (f32[128,512]{1,0:T(8,128)S(1)}, f32[128,512]{1,0:T(8,128)S(1)}, u32[]{:S(2)}, u32[]{:S(2)}) collective-permute-start(f32[128,512]{1,0:T(8,128)S(1)} %get-tuple-element.353), channel_id=1, source_target_pairs={{0,8},{1,9},{2,10},{3,11},{4,12},{5,13},{6,14},{7,15},{8,0},{9,1},... | collective-permute-start | bytes 786440 | tf_op jit(solution)/shard_map/ppermute | solution.py:709
  190.3 17.1 %collective-permute-start.25 = (f32[128,512]{1,0:T(8,128)S(1)}, f32[128,512]{1,0:T(8,128)S(1)}, u32[]{:S(2)}, u32[]{:S(2)}) collective-permute-start(f32[128,512]{1,0:T(8,128)S(1)} %add.35.own_ref), channel_id=1, source_target_pairs={{0,8},{1,9},{2,10},{3,11},{4,12},{5,13},{6,14},{7,15},{8,0},{9,1},... | collective-permute-start | bytes 786440 | tf_op jit(solution)/shard_map/ppermute | solution.py:709
  199.0 11.4 %collective-permute-start.27 = (f32[128,512]{1,0:T(8,128)S(1)}, f32[128,512]{1,0:T(8,128)S(1)}, u32[]{:S(2)}, u32[]{:S(2)}) collective-permute-start(f32[128,512]{1,0:T(8,128)S(1)} %add.36), channel_id=1, source_target_pairs={{0,16},{1,17},{2,18},{3,19},{4,20},{5,21},{6,22},{7,23},{8,24},{9,... | collective-permute-start | bytes 786440 | tf_op jit(solution)/shard_map/ppermute | solution.py:709
  213.0 14.6 %collective-permute-start.30 = (f32[256,512]{1,0:T(8,128)S(1)}, f32[256,512]{1,0:T(8,128)S(1)}, u32[]{:S(2)}, u32[]{:S(2)}) collective-permute-start(f32[256,512]{1,0:T(8,128)S(1)} %shard_map.320.own_ref), channel_id=1, source_target_pairs={{0,2},{1,5},{2,0},{3,7},{4,6},{5,1},{6,4},{7,3},{8,10},{9,13},{10,... | collective-permute-start | bytes 1572872 | tf_op jit(solution)/shard_map/ppermute | solution.py:709
  214.9 35.6 %collective-permute-start.38 = (f32[128,2048]{1,0:T(8,128)S(1)}, f32[128,2048]{1,0:T(8,128)S(1)}, u32[]{:S(2)}, u32[]{:S(2)}) collective-permute-start(f32[128,2048]{1,0:T(8,128)S(1)} %shard_map.322.own_ref), channel_id=1, source_target_pairs={{0,4},{1,3},{2,6},{3,1},{4,0},{5,7},{6,2},{7,5},{8,12},{9,11},{10,... | collective-permute-start | bytes 3145736 | tf_op jit(solution)/shard_map/ppermute | solution.py:709
  227.7 23.0 %collective-permute-start.40 = (f32[512,512]{1,0:T(8,128)S(1)}, f32[512,512]{1,0:T(8,128)S(1)}, u32[]{:S(2)}, u32[]{:S(2)}) collective-permute-start(f32[512,512]{1,0:T(8,128)S(1)} %shard_map.325.own_ref), channel_id=1, source_target_pairs={{0,4},{1,3},{2,6},{3,1},{4,0},{5,7},{6,2},{7,5},{8,12},{9,11},{10,... | collective-permute-start | bytes 3145736 | tf_op jit(solution)/shard_map/ppermute | solution.py:709
  228.7 8.7 %collective-permute-start.29 = (f32[128,512]{1,0:T(8,128)S(1)}, f32[128,512]{1,0:T(8,128)S(1)}, u32[]{:S(2)}, u32[]{:S(2)}) collective-permute-start(f32[128,512]{1,0:T(8,128)S(1)} %add.37.own_ref), channel_id=1, source_target_pairs={{0,8},{1,9},{2,10},{3,11},{4,12},{5,13},{6,14},{7,15},{8,0},{9,1},... | collective-permute-start | bytes 786440 | tf_op jit(solution)/shard_map/ppermute | solution.py:709
  237.5 12.8 %collective-permute-start.35 = (f32[256,512]{1,0:T(8,128)S(1)}, f32[256,512]{1,0:T(8,128)S(1)}, u32[]{:S(2)}, u32[]{:S(2)}) collective-permute-start(f32[256,512]{1,0:T(8,128)S(1)} %shard_map.327.own_ref), channel_id=1, source_target_pairs={{0,2},{1,5},{2,0},{3,7},{4,6},{5,1},{6,4},{7,3},{8,10},{9,13},{10,... | collective-permute-start | bytes 1572872 | tf_op jit(solution)/shard_map/ppermute | solution.py:709
  251.5 17.0 %collective-permute-start.36 = (f32[512,512]{1,0:T(8,128)S(1)}, f32[512,512]{1,0:T(8,128)S(1)}, u32[]{:S(2)}, u32[]{:S(2)}) collective-permute-start(f32[512,512]{1,0:T(8,128)S(1)} %shard_map.328.own_ref), channel_id=1, source_target_pairs={{0,4},{1,3},{2,6},{3,1},{4,0},{5,7},{6,2},{7,5},{8,12},{9,11},{10,... | collective-permute-start | bytes 3145736 | tf_op jit(solution)/shard_map/ppermute | solution.py:709
  252.4 15.6 %collective-permute-start.37 = (f32[320,128]{1,0:T(8,128)S(1)}, f32[320,128]{1,0:T(8,128)S(1)}, u32[]{:S(2)}, u32[]{:S(2)}) collective-permute-start(f32[320,128]{1,0:T(8,128)S(1)} %shard_map.326.own_ref), channel_id=1, source_target_pairs={{0,4},{1,3},{2,6},{3,1},{4,0},{5,7},{6,2},{7,5},{8,12},{9,11},{10,... | collective-permute-start | bytes 491528 | tf_op jit(solution)/shard_map/ppermute | solution.py:709
  (35 other events, 360.2 us)
